TPU v7x, 256 devices: a whole 4x4x8 slice. The times are simulated.
256 devices in a mesh: cfg: 2 (over core), blk: 16 (over z_hi, y), uly: 8 (over x, z_lo).
Axes of the slice: x: 4, y: 4, z: 8 (z_hi: 4, z_lo: 2; z = z_hi * 2 + z_lo), core: 2. Of those that a mesh axis runs over, the one named last changes fastest.
Arguments:
- hidden: bfloat16 [2, 10240, 2432], P('cfg', ('blk', 'uly')), may hold values from -6 to 6
- text_states: bfloat16 [2, 336, 2432], P('cfg', 'blk'), may hold values from -72 to 72
- modulation: float32 [2, 5, 2432], P('cfg'), may hold values from -3 to 3
- w_qkv: bfloat16 [3, 2432, 2048], P(None, None, 'uly'), may hold values from -0.125 to 0.125
- w_text: bfloat16 [2, 2432, 2048], P(None, None, 'uly'), may hold values from -0.125 to 0.125
- w_out: bfloat16 [2048, 2432], P('uly'), may hold values from -0.125 to 0.125
- qk_gain: float32 [2, 64], replicated, may hold values from 0.8 to 5
- w_final: bfloat16 [2432, 64], replicated, may hold values from -0.125 to 0.125
- w_patch: bfloat16 [64, 2432], replicated, may hold values from -0.75 to 0.75
- position: bfloat16 [10240, 2432], P(('blk', 'uly'), 'cfg'), may hold values from -6 to 6
- latent: float32 [10240, 64], P(('blk', 'uly')), may hold values from -6 to 6
- text_len: int32 [2], P('cfg'), may hold values from 84 to 336, as said below
- timestep: int32 [1], replicated, may hold values from 0 to 27
- sigma_table: int32 [29], replicated, may hold values from 0 to 1000, as said below
Outputs:
- guided: float32 [10240, 64], P(('blk', 'uly'), 'cfg')
- next_latent: float32 [10240, 64], P(('blk', 'uly'), 'cfg')
- next_hidden: bfloat16 [10240, 2432], P(('blk', 'uly'), 'cfg')
Inputs may be any that keep to these rules, and one draw needn't show every extreme that they name: `text_len`: entry 1 equals 336; entry 0 is at least 84. `sigma_table`: non-increasing, 1000 at index 0 and 0 at index 28.
All inputs are finite; a program needn't handle non-finite values.
Results may differ from a plain program's by a relative error of at most 0.012.
The roundings to bfloat16 on the way count: a program that leaves them out, or rounds other values in their place, can miss the bound.
Values may be sent and summed in bfloat16 or wider, within the bound.
A program may use at most 128 MiB of HBM per device.

v0:
```python
import jax
import jax.numpy as jnp
from jax import lax
from jax.sharding import PartitionSpec as P

HEAD = 64


guidance = 3.5
epsilon = 1e-06


def from_partner(value, axis, apart):
    return lax.ppermute(value, axis, [(i, i ^ 1 << apart) for i in range(lax.axis_size(axis))])


def layer_norm(values):
    average = jnp.mean(values, axis=-1, keepdims=True)
    centered = values - average
    spread = jnp.mean(centered * centered, axis=-1, keepdims=True)
    return centered * lax.rsqrt(spread + epsilon)


def rms_heads(values, gain):
    row_total = values.shape[0]
    head_count = values.shape[1] // HEAD
    split = values.reshape(row_total, head_count, HEAD)
    normed = split * lax.rsqrt(jnp.mean(split * split, axis=-1, keepdims=True) + epsilon) * gain
    return normed.reshape(row_total, head_count * HEAD).astype(jnp.bfloat16)


def body(
    hidden,
    text_states,
    modulation,
    w_qkv,
    w_text,
    w_out,
    qk_gain,
    w_final,
    w_patch,
    position,
    latent,
    text_len,
    timestep,
    sigma_table,
):
    states = hidden[0].astype(jnp.float32)
    branch_mod = modulation[0]
    modulated = (layer_norm(states) * (1.0 + branch_mod[1]) + branch_mod[0]).astype(jnp.bfloat16)
    pieces = lax.all_gather(modulated, "uly", axis=0, tiled=True)
    query_part = rms_heads(
        jnp.dot(pieces, w_qkv[0], preferred_element_type=jnp.float32), qk_gain[0]
    )
    key_part = rms_heads(jnp.dot(pieces, w_qkv[1], preferred_element_type=jnp.float32), qk_gain[1])
    value_part = jnp.dot(pieces, w_qkv[2], preferred_element_type=jnp.float32).astype(jnp.bfloat16)
    projected = jnp.stack([query_part, key_part, value_part])
    pieces = lax.all_gather(text_states[0], "blk", axis=0, tiled=True)
    key_part = rms_heads(jnp.dot(pieces, w_text[0], preferred_element_type=jnp.float32), qk_gain[1])
    value_part = jnp.dot(pieces, w_text[1], preferred_element_type=jnp.float32).astype(jnp.bfloat16)
    text_pair = jnp.stack([key_part, value_part])
    group_rows = projected.shape[1]
    width_local = projected.shape[2]
    head_count = width_local // HEAD
    score_scale = HEAD ** (-0.5)
    queries = projected[0].reshape(group_rows, head_count, HEAD)
    text_keys = text_pair[0].reshape(-1, head_count, HEAD)
    text_values = text_pair[1].reshape(-1, head_count, HEAD)
    usable = jnp.arange(text_keys.shape[0]) < text_len[0]
    scores = (
        jnp.einsum("qhd,khd->hqk", queries, text_keys, preferred_element_type=jnp.float32)
        * score_scale
    )
    scores = jnp.where(usable[None, None, :], scores, -1e30)
    highest = jnp.max(scores, axis=-1)
    weights = jnp.exp(scores - highest[..., None])
    totals = jnp.sum(weights, axis=-1)
    summed = jnp.einsum(
        "hqk,khd->hqd",
        weights.astype(jnp.bfloat16),
        text_values,
        preferred_element_type=jnp.float32,
    )

    def fold_block(running, key_block, value_block):
        run_max, run_total, run_sum = running
        block_scores = (
            jnp.einsum(
                "qhd,khd->hqk",
                queries,
                key_block.reshape(-1, head_count, HEAD),
                preferred_element_type=jnp.float32,
            )
            * score_scale
        )
        new_max = jnp.maximum(run_max, jnp.max(block_scores, axis=-1))
        shrink = jnp.exp(run_max - new_max)
        block_weights = jnp.exp(block_scores - new_max[..., None])
        new_total = run_total * shrink + jnp.sum(block_weights, axis=-1)
        new_sum = run_sum * shrink[..., None] + jnp.einsum(
            "hqk,khd->hqd",
            block_weights.astype(jnp.bfloat16),
            value_block.reshape(-1, head_count, HEAD),
            preferred_element_type=jnp.float32,
        )
        return (new_max, new_total, new_sum)

    key_rows = lax.all_gather(projected[1], "blk", axis=0, tiled=True)
    value_rows = lax.all_gather(projected[2], "blk", axis=0, tiled=True)
    block_count = key_rows.shape[0] // group_rows
    key_blocks = key_rows.reshape(block_count, group_rows, width_local)
    value_blocks = value_rows.reshape(block_count, group_rows, width_local)

    def scan_step(state, operands):
        return (fold_block(state, operands[0], operands[1]), None)

    result, unused = lax.scan(scan_step, (highest, totals, summed), (key_blocks, value_blocks))
    run_max, run_total, run_sum = result
    attended = (run_sum / run_total[..., None]).astype(jnp.bfloat16)
    attended = attended.transpose(1, 0, 2).reshape(group_rows, width_local)
    whole_out = lax.all_gather(w_out, "uly", axis=0, tiled=True)
    own_heads = lax.all_to_all(attended, "uly", split_axis=0, concat_axis=1, tiled=True)
    projected_out = jnp.dot(own_heads, whole_out, preferred_element_type=jnp.float32)
    mixed = states + branch_mod[2] * projected_out
    final = (layer_norm(mixed) * (1.0 + branch_mod[4]) + branch_mod[3]).astype(jnp.bfloat16)
    velocity = jnp.dot(final, w_final, preferred_element_type=jnp.float32)
    partner = from_partner(velocity, "cfg", 0)
    branch_index = lax.axis_index("cfg")
    is_cond = branch_index == 0
    cond_velocity = jnp.where(is_cond, velocity, partner)
    uncond_velocity = jnp.where(is_cond, partner, velocity)
    guided = uncond_velocity + guidance * (cond_velocity - uncond_velocity)
    sigmas = sigma_table.astype(jnp.float32) / 1000.0
    levels = jnp.arange(sigmas.shape[0], dtype=jnp.int32)
    sigma_now = jnp.sum(jnp.where(levels == timestep[0], sigmas, 0.0))
    sigma_next = jnp.sum(jnp.where(levels == timestep[0] + 1, sigmas, 0.0))
    next_latent = latent + (sigma_next - sigma_now) * guided
    feature_half = position.shape[1]
    patch_columns = lax.dynamic_slice_in_dim(w_patch, branch_index * feature_half, feature_half, 1)
    embedded = jnp.dot(
        next_latent.astype(jnp.bfloat16), patch_columns, preferred_element_type=jnp.float32
    )
    next_hidden = (embedded + position.astype(jnp.float32)).astype(jnp.bfloat16)
    channel_half = latent.shape[1] // 2
    guided_own = lax.dynamic_slice_in_dim(guided, branch_index * channel_half, channel_half, 1)
    latent_own = lax.dynamic_slice_in_dim(next_latent, branch_index * channel_half, channel_half, 1)
    return (guided_own, latent_own, next_hidden)


def solution(mesh):
    in_specs = (
        P("cfg", ("blk", "uly"), None),
        P("cfg", "blk", None),
        P("cfg", None, None),
        P(None, None, "uly"),
        P(None, None, "uly"),
        P("uly", None),
        P(),
        P(),
        P(),
        P(("blk", "uly"), "cfg"),
        P(("blk", "uly"), None),
        P("cfg"),
        P(),
        P(),
    )
    out_specs = (P(("blk", "uly"), "cfg"), P(("blk", "uly"), "cfg"), P(("blk", "uly"), "cfg"))
    return jax.shard_map(body, mesh=mesh, in_specs=in_specs, out_specs=out_specs, check_vma=False)
```

profile of v0, /device:TPU:3, one launch (start us, length us, event | category | flops | bytes accessed | tf_op | source)
XLA Modules:
  0.0 558.6 jit_solution(10090107653195136931)
XLA Ops:
  18.0 69.9 %all-gather.7.cloned.1.call-done = bf16[640,2432]{1,0:T(8,128)(2,1)} async-done(((bf16[80,2432]{1,0:T(8,128)(2,1)}), bf16[640,2432]{1,0:T(8,128)(2,1)}) %all-gather.7.cloned.1.call-update) | async-done | bytes 3112976 | tf_op jit(solution)/shard_map/all_gather | solution.py:51
  101.5 59.1 %all-gather.15.cloned.1.call-done = bf16[1,336,2432]{2,0,1:T(2,128)(2,1)} async-done(((bf16[1,21,2432]{2,0,1:T(2,128)(2,1)}), bf16[1,336,2432]{2,0,1:T(2,128)(2,1)}) %all-gather.15.cloned.1.call-update) | async-done | bytes 1634320 | tf_op jit(solution)/shard_map/all_gather | solution.py:58
  172.5 70.0 %all-gather.9.cloned.1.call-done = bf16[10240,256]{1,0:T(8,128)(2,1)} async-done(((bf16[640,256]{1,0:T(8,128)(2,1)}), bf16[10240,256]{1,0:T(8,128)(2,1)}) %all-gather.9.cloned.1.call-update) | async-done | bytes 5242896 | tf_op jit(solution)/shard_map/all_gather | solution.py:108
  242.5 88.4 %all-gather.11.cloned.1.call-done = bf16[10240,256]{1,0:T(8,128)(2,1)} async-done(((bf16[640,256]{1,0:T(8,128)(2,1)}), bf16[10240,256]{1,0:T(8,128)(2,1)}) %all-gather.11.cloned.1.call-update) | async-done | bytes 5242896 | tf_op jit(solution)/shard_map/all_gather | solution.py:109
  330.9 171.9 %while.14 = (s32[]{:T(128)}, f32[4,640]{1,0:T(4,128)S(1)}, f32[4,640]{1,0:T(4,128)S(1)}, f32[4,640,64]{1,2,0:T(8,128)S(1)}, bf16[16,640,256]{2,1,0:T(8,128)(2,1)...) while((s32[]{:T(128)}, f32[4,640]{1,0:T(4,128)S(1)}, ...), condition=%wide.region_10.11_spmd, body=%wide.region_7.10_spmd.sunk | while | flops 432870400 | bytes 50954356 | solution.py:117
  348.0 4.7 fusion.89
  359.1 4.3 fusion.89
  369.8 4.3 fusion.89
  380.5 4.3 fusion.89
  391.2 4.3 fusion.89
  402.0 4.3 fusion.89
  412.7 4.3 fusion.89
  423.4 4.3 fusion.89
  434.1 4.3 fusion.89
  444.9 4.3 fusion.89
  455.6 4.3 fusion.89
  466.3 4.3 fusion.89
  477.0 4.3 fusion.89
  487.8 4.3 fusion.89
  498.5 4.3 fusion.89
  504.5 11.2 %all-to-all-start = ((bf16[8,80,256]{2,1,0:T(8,128)(2,1)}), bf16[8,80,256]{2,1,0:T(8,128)(2,1)S(1)}, u32[]{:S(2)}, u32[]{:S(2)}) async-start(bf16[8,80,256]{2,1,0:T(8,128)(2,1)} %copy.52), calls=%async_computation | async-start | bytes 655360 | tf_op jit(solution)/shard_map/all_to_all | solution.py:122
  516.4 8.5 %all-to-all-done = bf16[8,80,256]{2,1,0:T(8,128)(2,1)S(1)} async-done(((bf16[8,80,256]{2,1,0:T(8,128)(2,1)}), bf16[8,80,256]{2,1,0:T(8,128)(2,1)S(1)}, u32[]{:S(2)}, u32[]{:S(2)}) %all-to-all-start) | async-done | bytes 327712 | tf_op jit(solution)/shard_map/all_to_all | solution.py:122
  525.0 16.2 %all-gather.13.cloned.1.call-done = bf16[2048,2432]{1,0:T(8,128)(2,1)} async-done(((bf16[256,2432]{1,0:T(8,128)(2,1)}), bf16[2048,2432]{1,0:T(8,128)(2,1)}) %all-gather.13.cloned.1.call-update) | async-done | bytes 9961488 | tf_op jit(solution)/shard_map/all_gather | solution.py:121
  541.2 5.8 %fusion.65 = (f32[80]{0:T(128)S(1)}, f32[80,2432]{1,0:T(8,128)S(1)}) fusion(bf16[80,2048]{1,0:T(8,128)(2,1)S(1)} %bitcast.126, bf16[2048,2432]{1,0:T(8,128)(2,1)} %all-gather.13.cloned.1.call-done, f32[2432]{0:T(1024)S(1)} %get-tuple-element.74, bf16[1,80,2432]{2,1,0:T(8,128)(2,1)S(1)} %copy-done.2), kind=kOutput, calls=%fused_computation.101 | convolution fusion | flops 797695936 | bytes 11466560 | tf_op jit(solution)/shard_map/dot_general | solution.py:123
  (230 shorter events, 147.0 us)
Async XLA Ops:
  7.2 543.9 %copy-start = (bf16[64,2432]{1,0:T(8,128)(2,1)S(1)}, bf16[64,2432]{1,0:T(8,128)(2,1)}, u32[]{:S(2)}) copy-start(bf16[64,2432]{1,0:T(8,128)(2,1)} %param.24) | copy-start | bytes 933892
  7.2 80.7 %all-gather.7.cloned.1.call-start = ((), (), s32[]{:S(2)}) async-start(), calls=%async_computation.1 | async-start | bytes 3502080 | tf_op jit(solution)/shard_map/all_gather | solution.py:51
  12.7 147.9 %all-gather.15.cloned.1.call-start = ((), (), s32[]{:S(2)}) async-start(), calls=%async_computation.5 | async-start | bytes 3472896 | tf_op jit(solution)/shard_map/all_gather | solution.py:58
  14.5 3.5 copy-start.7
  14.5 228.0 %all-gather.9.cloned.1.call-start = ((), (), s32[]{:S(2)}) async-start(), calls=%async_computation.2 | async-start | bytes 5570560 | tf_op jit(solution)/shard_map/all_gather | solution.py:108
  92.4 238.5 %all-gather.11.cloned.1.call-start = ((), (), s32[]{:S(2)}) async-start(), calls=%async_computation.3 | async-start | bytes 5570560 | tf_op jit(solution)/shard_map/all_gather | solution.py:109
  96.4 444.8 %all-gather.13.cloned.1.call-start = ((), (), s32[]{:S(2)}) async-start(), calls=%async_computation.4 | async-start | bytes 11206656 | tf_op jit(solution)/shard_map/all_gather | solution.py:121
  160.6 3.3 copy-start.3
  355.1 2.7 copy-start.1
  376.5 2.7 copy-start.1
  387.3 2.7 copy-start.1
  398.0 2.7 copy-start.1
  408.7 2.7 copy-start.1
  419.4 2.7 copy-start.1
  430.1 2.7 copy-start.1
  440.9 2.7 copy-start.1
  451.6 2.7 copy-start.1
  502.8 38.4 %copy-start.2 = (bf16[1,80,2432]{2,1,0:T(8,128)(2,1)S(1)}, bf16[1,80,2432]{2,1,0:T(8,128)(2,1)}, u32[]{:S(2)}) copy-start(bf16[1,80,2432]{2,1,0:T(8,128)(2,1)} %param.16) | copy-start | bytes 1167364
  504.5 20.4 %all-to-all-start = ((bf16[8,80,256]{2,1,0:T(8,128)(2,1)}), bf16[8,80,256]{2,1,0:T(8,128)(2,1)S(1)}, u32[]{:S(2)}, u32[]{:S(2)}) async-start(bf16[8,80,256]{2,1,0:T(8,128)(2,1)} %copy.52), calls=%async_computation | async-start | bytes 655360 | tf_op jit(solution)/shard_map/all_to_all | solution.py:122
  541.2 6.1 %copy-start.4 = (bf16[2432,64]{0,1:T(8,128)(2,1)S(1)}, bf16[2432,64]{0,1:T(8,128)(2,1)}, u32[]{:S(2)}) copy-start(bf16[2432,64]{0,1:T(8,128)(2,1)} %param.23) | copy-start | bytes 933892
  541.2 7.3 %copy-start.8 = (s32[29]{0:T(128)S(1)}, s32[29]{0:T(128)}, u32[]{:S(2)}) copy-start(s32[29]{0:T(128)} %param.29) | copy-start | bytes 352
  541.2 9.2 %copy-start.6 = (f32[80,64]{0,1:T(8,128)S(1)}, f32[80,64]{0,1:T(8,128)}, u32[]{:S(2)}) copy-start(f32[80,64]{0,1:T(8,128)} %param.26) | copy-start | bytes 61444
  541.2 9.9 %copy-start.5 = (bf16[80,1216]{1,0:T(8,128)(2,1)S(1)}, bf16[80,1216]{1,0:T(8,128)(2,1)}, u32[]{:S(2)}) copy-start(bf16[80,1216]{1,0:T(8,128)(2,1)} %param.25) | copy-start | bytes 583684
  547.7 2.7 collective-permute-start
  (7 other events, 18.7 us)
Sparse Core Ops, SparseCore 0:
  12.8 75.0 all-gather.6
  90.8 69.7 all-gather.14
  163.0 79.3 all-gather.8
  244.8 86.0 all-gather.10
  332.5 208.6 all-gather.12
where the time goes:
time: 561 us; the launch traced here: 559 us
  waiting for transfers between devices  313 us (56%)
  matrix products  112 us (20%)
  local copies, waits for them, and re-layouts  79.3 us (14%)
  other arithmetic  25.1 us (4%)
  between operations  16.6 us (3%)
  starting transfers between devices  12.4 us (2%)
    all_gather x1, waiting for transfers between devices, body(): value_rows = lax.all_gather(projected[2], 'blk', axis=0, tiled=True)  88.4 us
    all_gather x1, waiting for transfers between devices, body(): key_rows = lax.all_gather(projected[1], 'blk', axis=0, tiled=True)  70 us
    all_gather x1, waiting for transfers between devices, body(): pieces = lax.all_gather(modulated, 'uly', axis=0, tiled=True)  69.9 us
    dot_general x16, matrix products, fold_block(): jnp.einsum('hqk,khd->hqd', block_weights.astype(jnp.bfloat16), value_bloc...  68.9 us
    all_gather x1, waiting for transfers between devices, body(): pieces = lax.all_gather(text_states[0], 'blk', axis=0, tiled=True)  59.1 us
    while x48, local copies, waits for them, and re-layouts  42.6 us
    dynamic_slice x48, local copies, waits for them, and re-layouts, body(): lax.scan(scan_step, (highest, totals, summed), (key_blocks, value_blocks))  24.4 us
    reduce_sum x16, other arithmetic, fold_block(): new_total = run_total * shrink + jnp.sum(block_weights, axis=-1)  17.3 us
  transfers between devices with their start and end apart: 7, of which 6 were waited for; matrix products, arithmetic and copies ran while one was open for 29% of the time, Pallas kernels for 0%

commit v1 on v0

v1 whole, which is shorter than its diff:
```python
import functools

import jax
import jax.numpy as jnp
import numpy as np
from jax import lax
from jax.experimental import pallas as pl
from jax.experimental.pallas import tpu as pltpu
from jax.sharding import PartitionSpec as P

HEAD = 64
guidance = 3.5
epsilon = 1e-06
MESH = pl.DeviceIdType.MESH
bf16 = jnp.bfloat16
f32 = jnp.float32

ROWS = 80
PAIR = 160
TXT_ROWS = 21
TXT_PAD = 32
FIRST = 48


def layer_norm(values):
    average = jnp.mean(values, axis=-1, keepdims=True)
    centered = values - average
    spread = jnp.mean(centered * centered, axis=-1, keepdims=True)
    return centered * lax.rsqrt(spread + epsilon)


def coords():
    c = lax.axis_index("cfg")
    b = lax.axis_index("blk")
    u = lax.axis_index("uly")
    return c, b // 4, b % 4, u // 2, u % 2


def head_norm(values, gain):
    rows = values.shape[0]
    low = lax.broadcasted_iota(jnp.int32, (rows, 128), 1) < HEAD
    columns = []
    for t in range(2):
        x = values[:, 128 * t : 128 * t + 128]
        sq = x * x
        a = jnp.sum(jnp.where(low, sq, 0.0), axis=1, keepdims=True)
        b = jnp.sum(jnp.where(low, 0.0, sq), axis=1, keepdims=True)
        scale = lax.rsqrt(jnp.where(low, a, b) * (1.0 / HEAD) + epsilon)
        columns.append(x * scale * gain)
    return columns


def pack_heads(left, right):
    rows = left[0].shape[0]
    low = lax.broadcasted_iota(jnp.int32, (rows, 128), 1) < HEAD
    out = []
    for t in range(2):
        out.append(jnp.where(low, left[t], pltpu.roll(right[t], HEAD, 1)))
        out.append(jnp.where(low, pltpu.roll(left[t], HEAD, 1), right[t]))
    return out


def project_kernel(
    hid_ref, txt_ref, mod_ref, wqkv_ref, wtext_ref, gain_ref,
    kv_ref, tkv_ref, q_ref,
    mods, wq, wt, txt, kvst, qst, tst,
    wsem, lsem, bsend, brecv, zsend, zrecv, qsend, qrecv, ysend, yrecv,
    tzsend, tzrecv, tysend, tyrecv,
):
    c, zh, y, x, zl = coords()
    u = x * 2 + zl
    blk = zh * 4 + y

    def at(zh_=None, y_=None, x_=None, zl_=None):
        zz = zh if zh_ is None else lax.rem(zh + zh_, 4)
        yy = y if y_ is None else lax.rem(y + y_, 4)
        xx = x if x_ is None else lax.rem(x + x_, 4)
        ll = zl if zl_ is None else 1 - zl
        return (c, zz * 4 + yy, xx * 2 + ll)

    partner = at(zl_=1)
    up, down = at(x_=1), at(x_=3)

    wcopies = []
    for i in range(3):
        wcopies.append(pltpu.make_async_copy(wqkv_ref.at[i], wq.at[i], wsem.at[i]))
    for i in range(2):
        wcopies.append(pltpu.make_async_copy(wtext_ref.at[i], wt.at[i], wsem.at[3 + i]))
    for w in wcopies[3:] + wcopies[:3]:
        w.start()

    barrier = pltpu.get_barrier_semaphore()
    peers = [partner, up, down] + [at(zh_=d) for d in (1, 2, 3)] + [at(y_=d) for d in (1, 2, 3)]
    for peer in peers:
        pl.semaphore_signal(barrier, inc=1, device_id=peer, device_id_type=MESH)

    states = hid_ref[0].astype(f32)
    modulated = layer_norm(states) * (1.0 + mod_ref[0, 1:2, :]) + mod_ref[0, 0:1, :]
    mods[u] = modulated.astype(bf16)
    txt[...] = jnp.zeros_like(txt)
    txt[0:TXT_ROWS, :] = txt_ref[0]
    pl.semaphore_wait(barrier, len(peers))

    def remote(src, dst, send, recv, to):
        return pltpu.make_async_remote_copy(
            src_ref=src, dst_ref=dst, send_sem=send, recv_sem=recv,
            device_id=to, device_id_type=MESH,
        )

    def shard(i, x_, zl_, part, to):
        s = lax.rem(x + x_, 4) * 2 + (zl if zl_ == 0 else 1 - zl)
        ref = mods.at[s]
        if part == 1:
            ref = mods.at[s, pl.ds(0, FIRST)]
        elif part == 2:
            ref = mods.at[s, pl.ds(FIRST, ROWS - FIRST)]
        return remote(ref, ref, bsend.at[i], brecv.at[i], to)

    sends = {
        0: shard(0, 0, 0, 0, partner),
        1: shard(1, 0, 0, 0, up),
        2: shard(2, 0, 0, 0, down),
        3: shard(3, 0, 1, 0, up),
        4: shard(4, 0, 1, 0, down),
        5: shard(5, 3, 0, 1, up),
        6: shard(6, 1, 0, 2, down),
        7: shard(7, 3, 1, 1, up),
        8: shard(8, 1, 1, 2, down),
    }
    arrive = {
        0: shard(0, 0, 1, 0, partner),
        1: shard(1, 3, 0, 0, up),
        2: shard(2, 1, 0, 0, down),
        3: shard(3, 3, 1, 0, up),
        4: shard(4, 1, 1, 0, down),
        5: shard(5, 2, 0, 1, up),
        6: shard(6, 2, 0, 2, down),
        7: shard(7, 2, 1, 1, up),
        8: shard(8, 2, 1, 2, down),
    }
    for i in (0, 1, 2):
        sends[i].start()

    gain_q = gain_ref[0:1, :]
    gain_k = gain_ref[1:2, :]

    def copy_kv(t, p, d):
        h = lax.rem(zh + d, 4)
        return remote(kvst.at[t, h], kv_ref.at[blk, p], zsend.at[t, d - 1], zrecv.at[t, d - 1], at(zh_=d))

    def copy_q(t, p, d):
        h = lax.rem(zh + d, 4)
        return remote(qst.at[t, h], q_ref.at[zh, p], qsend.at[t, d - 1], qrecv.at[t, d - 1], at(zh_=d))

    def landed_kv(t, p, d):
        slot = kv_ref.at[lax.rem(zh + 4 - d, 4) * 4 + y, p]
        return remote(slot, slot, zsend.at[t, d - 1], zrecv.at[t, d - 1], at(zh_=d))

    def landed_q(t, p, d):
        slot = q_ref.at[lax.rem(zh + 4 - d, 4), p]
        return remote(slot, slot, qsend.at[t, d - 1], qrecv.at[t, d - 1], at(zh_=d))

    def copy_y(t, p, d, e):
        if d == 0:
            src, dst = kvst.at[t, zh], kv_ref.at[blk, p]
        else:
            src = dst = kv_ref.at[lax.rem(zh + 4 - d, 4) * 4 + y, p]
        return remote(src, dst, ysend.at[t, d, e - 1], yrecv.at[t, d, e - 1], at(y_=e))

    def landed_y(t, p, d, e):
        slot = kv_ref.at[lax.rem(zh + 4 - d, 4) * 4 + lax.rem(y + 4 - e, 4), p]
        return remote(slot, slot, ysend.at[t, d, e - 1], yrecv.at[t, d, e - 1], at(y_=e))

    def text_z(d):
        h = lax.rem(zh + d, 4)
        return remote(tst.at[h], tkv_ref.at[blk], tzsend.at[d - 1], tzrecv.at[d - 1], at(zh_=d))

    def text_z_landed(d):
        slot = tkv_ref.at[lax.rem(zh + 4 - d, 4) * 4 + y]
        return remote(slot, slot, tzsend.at[d - 1], tzrecv.at[d - 1], at(zh_=d))

    def text_y(d, e):
        if d == 0:
            src, dst = tst.at[zh], tkv_ref.at[blk]
        else:
            src = dst = tkv_ref.at[lax.rem(zh + 4 - d, 4) * 4 + y]
        return remote(src, dst, tysend.at[d, e - 1], tyrecv.at[d, e - 1], at(y_=e))

    def text_y_landed(d, e):
        slot = tkv_ref.at[lax.rem(zh + 4 - d, 4) * 4 + lax.rem(y + 4 - e, 4)]
        return remote(slot, slot, tysend.at[d, e - 1], tyrecv.at[d, e - 1], at(y_=e))

    for w in wcopies[3:]:
        w.wait()
    rows = txt[...]
    tk = head_norm(jnp.dot(rows, wt[0], preferred_element_type=f32), gain_k)
    tv = jnp.dot(rows, wt[1], preferred_element_type=f32)
    for h, value in enumerate(pack_heads(tk, [tv[:, 0:128], tv[:, 128:256]])):
        tst[h] = value.astype(bf16)
    for d in (1, 2, 3):
        text_z(d).start()
    for e in (1, 2, 3):
        text_y(0, e).start()
    local_text = pltpu.make_async_copy(tst.at[zh], tkv_ref.at[blk], lsem.at[8])
    local_text.start()

    for w in wcopies[:3]:
        w.wait()

    def project(t, x_):
        p = lax.rem(x + x_, 4)
        pair = mods[pl.ds(p * 2, 2)].reshape(PAIR, mods.shape[2])
        qs = head_norm(jnp.dot(pair, wq[0], preferred_element_type=f32), gain_q)
        for h, value in enumerate(pack_heads([v[0:ROWS] for v in qs], [v[ROWS:PAIR] for v in qs])):
            qst[t, h] = value.astype(bf16)
        ks = head_norm(jnp.dot(pair, wq[1], preferred_element_type=f32), gain_k)
        vs = jnp.dot(pair, wq[2], preferred_element_type=f32)
        for h, value in enumerate(pack_heads(ks, [vs[:, 0:128], vs[:, 128:256]])):
            kvst[t, h] = value.astype(bf16)
        for d in (2, 1, 3):
            copy_kv(t, p, d).start()
        for d in (2, 1, 3):
            copy_q(t, p, d).start()
        for e in (2, 1, 3):
            copy_y(t, p, 0, e).start()
        pltpu.make_async_copy(kvst.at[t, zh], kv_ref.at[blk, p], lsem.at[t]).start()
        pltpu.make_async_copy(qst.at[t, zh], q_ref.at[zh, p], lsem.at[4 + t]).start()

    def pass_on(t, x_):
        p = lax.rem(x + x_, 4)
        for d in (1, 3, 2):
            landed_kv(t, p, d).wait_recv()
            for e in (2, 1, 3):
                copy_y(t, p, d, e).start()

    arrive[0].wait_recv()
    sends[3].start()
    sends[4].start()
    arrive[1].wait_recv()
    sends[5].start()
    arrive[2].wait_recv()
    sends[6].start()
    project(0, 0)
    for d in (1, 2, 3):
        text_z_landed(d).wait_recv()
        for e in (1, 2, 3):
            text_y(d, e).start()
    arrive[3].wait_recv()
    sends[7].start()
    arrive[4].wait_recv()
    sends[8].start()
    project(1, 3)
    project(2, 1)
    pass_on(0, 0)
    for i in (5, 6, 7, 8):
        arrive[i].wait_recv()
    project(3, 2)
    pass_on(1, 3)
    pass_on(2, 1)
    pass_on(3, 2)

    for i in range(9):
        sends[i].wait_send()
    local_text.wait()
    for d in (1, 2, 3):
        text_z(d).wait_send()
    for d in range(4):
        for e in (1, 2, 3):
            text_y(d, e).wait_send()
            text_y_landed(d, e).wait_recv()
    for t, x_ in enumerate((0, 3, 1, 2)):
        p = lax.rem(x + x_, 4)
        pltpu.make_async_copy(kvst.at[t, zh], kv_ref.at[blk, p], lsem.at[t]).wait()
        pltpu.make_async_copy(qst.at[t, zh], q_ref.at[zh, p], lsem.at[4 + t]).wait()
        for d in (1, 2, 3):
            copy_kv(t, p, d).wait_send()
            copy_q(t, p, d).wait_send()
            landed_q(t, p, d).wait_recv()
        for d in range(4):
            for e in (1, 2, 3):
                copy_y(t, p, d, e).wait_send()
                landed_y(t, p, d, e).wait_recv()


def project_heads(hidden, text_states, modulation, w_qkv, w_text, gains):
    width = hidden.shape[2]
    vmem = pl.BlockSpec(memory_space=pltpu.VMEM)
    hbm = pl.BlockSpec(memory_space=pl.ANY)
    dma = pltpu.SemaphoreType.DMA
    return pl.pallas_call(
        project_kernel,
        out_shape=[
            jax.ShapeDtypeStruct((16, 4, PAIR, 128), bf16),
            jax.ShapeDtypeStruct((16, TXT_PAD, 128), bf16),
            jax.ShapeDtypeStruct((4, 4, ROWS, 128), bf16),
        ],
        in_specs=[vmem, vmem, vmem, hbm, hbm, vmem],
        out_specs=[hbm, hbm, hbm],
        scratch_shapes=[
            pltpu.VMEM((8, ROWS, width), bf16),
            pltpu.VMEM((3, width, 256), bf16),
            pltpu.VMEM((2, width, 256), bf16),
            pltpu.VMEM((TXT_PAD, width), bf16),
            pltpu.VMEM((4, 4, PAIR, 128), bf16),
            pltpu.VMEM((4, 4, ROWS, 128), bf16),
            pltpu.VMEM((4, TXT_PAD, 128), bf16),
            dma((5,)),
            dma((9,)),
            dma((9,)), dma((9,)),
            dma((4, 3)), dma((4, 3)),
            dma((4, 3)), dma((4, 3)),
            dma((4, 4, 3)), dma((4, 4, 3)),
            dma((3,)), dma((3,)),
            dma((4, 3)), dma((4, 3)),
        ],
        compiler_params=pltpu.CompilerParams(
            collective_id=0, has_side_effects=True, vmem_limit_bytes=40 << 20
        ),
        name="project_heads",
    )(hidden, text_states, modulation, w_qkv, w_text, gains)


KEYS = 2560


def attend_kernel(len_ref, q_ref, kv_ref, tkv_ref, o_ref, q2, v1):
    step = pl.program_id(0)
    image = kv_ref.shape[0]
    text = tkv_ref.shape[0]

    @pl.when(step == 0)
    def _():
        def values_and_ones(block):
            wide = block.astype(f32)
            lane = lax.broadcasted_iota(jnp.int32, wide.shape, 1)
            return jnp.where(lane < HEAD, pltpu.roll(wide, HEAD, 1), 1.0).astype(bf16)

        @pl.loop(0, image // 512)
        def _(n):
            rows = pl.ds(pl.multiple_of(n * 512, 512), 512)
            v1[rows, :] = values_and_ones(kv_ref[rows, :])

        v1[image : image + text, :] = values_and_ones(tkv_ref[...])

    low = lax.broadcasted_iota(jnp.int32, (ROWS, 128), 1) < HEAD
    for p in range(4):
        packed = q_ref[0, p].astype(f32)
        q2[PAIR * p : PAIR * p + ROWS, :] = jnp.where(low, packed, 0.0).astype(bf16)
        q2[PAIR * p + ROWS : PAIR * p + PAIR, :] = jnp.where(
            low, pltpu.roll(packed, HEAD, 1), 0.0
        ).astype(bf16)
    q = q2[...]

    def fold(carry, keys, values, usable):
        top, acc = carry
        scores = lax.dot_general(q, keys, (((1,), (1,)), ((), ())), preferred_element_type=f32)
        if usable is not None:
            scores = jnp.where(usable, scores, -1e30)
        new_top = jnp.maximum(top, jnp.max(scores, axis=1, keepdims=True))
        weights = jnp.exp2(scores - new_top).astype(bf16)
        shrink = jnp.exp2(top - new_top)
        return new_top, acc * shrink + jnp.dot(weights, values, preferred_element_type=f32)

    count = q.shape[0]
    carry = (jnp.full((count, 1), -1e30, f32), jnp.zeros((count, 128), f32))

    def image_step(j, carry):
        rows = pl.ds(pl.multiple_of(j * KEYS, KEYS), KEYS)
        return fold(carry, kv_ref[rows, :], v1[rows, :], None)

    carry = lax.fori_loop(0, image // KEYS, image_step, carry)
    row = lax.broadcasted_iota(jnp.int32, (1, text), 1)
    block = row // TXT_PAD
    within = row - block * TXT_PAD
    usable = jnp.logical_and(within < TXT_ROWS, block * TXT_ROWS + within < len_ref[0])
    top, acc = fold(carry, tkv_ref[...], v1[image : image + text, :], usable)
    out = acc / acc[:, HEAD : HEAD + 1]
    high = pltpu.roll(out, HEAD, 1)
    low = lax.broadcasted_iota(jnp.int32, (FIRST, 128), 1) < HEAD
    for s in range(8):
        o_ref[0, s] = jnp.where(
            low,
            out[ROWS * s : ROWS * s + FIRST],
            high[ROWS * (s + 1) - FIRST : ROWS * (s + 1)],
        ).astype(bf16)


def attend(text_len, q, kv, tkv):
    image, text = kv.shape[0], tkv.shape[0]
    return pl.pallas_call(
        attend_kernel,
        grid=(4,),
        in_specs=[
            pl.BlockSpec(memory_space=pltpu.SMEM),
            pl.BlockSpec((1, 4, ROWS, 128), lambda i: (i, 0, 0, 0)),
            pl.BlockSpec((image, 128), lambda i: (0, 0)),
            pl.BlockSpec((text, 128), lambda i: (0, 0)),
        ],
        out_specs=pl.BlockSpec((1, 8, FIRST, 128), lambda i: (i, 0, 0, 0)),
        out_shape=jax.ShapeDtypeStruct((4, 8, FIRST, 128), bf16),
        scratch_shapes=[
            pltpu.VMEM((4 * PAIR, 128), bf16),
            pltpu.VMEM((image + text, 128), bf16),
        ],
        compiler_params=pltpu.CompilerParams(vmem_limit_bytes=44 << 20),
        cost_estimate=pl.CostEstimate(
            flops=4 * 4 * 4 * PAIR * (image + text) * 128,
            bytes_accessed=3 * image * 128 * 2,
            transcendentals=4 * 4 * PAIR * (image + text),
        ),
        name="attend",
    )(text_len, q, kv, tkv)


def finish_kernel(
    o_ref, hid_ref, mod_ref, wout_ref, wfinal_ref, wpatch_ref, pos_ref, lat_ref, time_ref, sigma_ref,
    guided_ref, latent_ref, next_ref,
    got, att, wo, vel, wsem, lsem, osend, orecv, vsend, vrecv,
):
    c, zh, y, x, zl = coords()
    u = x * 2 + zl
    load = pltpu.make_async_copy(wout_ref, wo, wsem.at[0])
    load.start()

    barrier = pltpu.get_barrier_semaphore()
    peers = []
    for k in range(1, 32):
        dz, du = k // 8, k % 8
        peers.append((c, lax.rem(zh + dz, 4) * 4 + y, lax.rem(u + du, 8)))
    other = (1 - c, zh * 4 + y, u)
    for peer in peers + [other]:
        pl.semaphore_signal(barrier, inc=1, device_id=peer, device_id_type=MESH)
    pl.semaphore_wait(barrier, len(peers) + 1)

    def remote(src, dst, send, recv, to):
        return pltpu.make_async_remote_copy(
            src_ref=src, dst_ref=dst, send_sem=send, recv_sem=recv,
            device_id=to, device_id_type=MESH,
        )

    def out_copy(k):
        dz, du = k // 8, k % 8
        z2, u2 = lax.rem(zh + dz, 4), lax.rem(u + du, 8)
        return remote(
            o_ref.at[z2, u2], got.at[u, zh], osend.at[k], orecv.at[k], peers[k - 1]
        )

    def in_copy(k):
        dz, du = k // 8, k % 8
        z2, u2 = lax.rem(zh + 4 - dz, 4), lax.rem(u + 8 - du, 8)
        slot = got.at[u2, z2]
        return remote(slot, slot, osend.at[k], orecv.at[k], peers[k - 1])

    for k in range(31, 0, -1):
        out_copy(k).start()
    own = pltpu.make_async_copy(o_ref.at[zh, u], got.at[u, zh], lsem.at[0])
    own.start()

    states = hid_ref[0].astype(f32)
    is_cond = c == 0
    half = pos_ref.shape[1]
    patch = wpatch_ref[...].astype(f32)
    patch = jnp.where(is_cond, patch[:, 0:half], patch[:, half : 2 * half]).astype(bf16)
    t = time_ref[0]
    sigma_now = sigma_ref[t].astype(f32) / 1000.0
    sigma_next = sigma_ref[t + 1].astype(f32) / 1000.0

    own.wait()
    for k in range(1, 32):
        in_copy(k).wait_recv()
    low = lax.broadcasted_iota(jnp.int32, (FIRST, 128), 1) < HEAD
    for s in range(8):
        for pair in range(2):
            even = got[s, 2 * pair].astype(f32)
            odd = got[s, 2 * pair + 1].astype(f32)
            columns = pl.ds(s * 256 + pair * 128, 128)
            att[0:FIRST, columns] = jnp.where(low, even, pltpu.roll(odd, HEAD, 1)).astype(bf16)
            rest = jnp.where(low, pltpu.roll(even, HEAD, 1), odd).astype(bf16)
            att[FIRST:ROWS, columns] = rest[2 * FIRST - ROWS : FIRST]
    load.wait()
    projected = jnp.dot(att[...], wo[...], preferred_element_type=f32)
    mixed = states + mod_ref[0, 2:3, :] * projected
    final = (layer_norm(mixed) * (1.0 + mod_ref[0, 4:5, :]) + mod_ref[0, 3:4, :]).astype(bf16)
    velocity = jnp.dot(final, wfinal_ref[...], preferred_element_type=f32)
    vel[0] = velocity
    exchange = remote(vel.at[0], vel.at[1], vsend.at[0], vrecv.at[0], other)
    exchange.start()
    exchange.wait()
    partner = vel[1]
    cond = jnp.where(is_cond, velocity, partner)
    uncond = jnp.where(is_cond, partner, velocity)
    guided = uncond + guidance * (cond - uncond)
    latent = lat_ref[...] + (sigma_next - sigma_now) * guided
    embedded = jnp.dot(latent.astype(bf16), patch, preferred_element_type=f32)
    next_ref[...] = (embedded + pos_ref[...].astype(f32)).astype(bf16)
    channels = guided_ref.shape[1]
    guided_ref[...] = jnp.where(is_cond, guided[:, 0:channels], guided[:, channels:])
    latent_ref[...] = jnp.where(is_cond, latent[:, 0:channels], latent[:, channels:])
    for k in range(1, 32):
        out_copy(k).wait_send()


def finish(o, hidden, modulation, whole_out, w_final, w_patch, position, latent, timestep, sigma_table):
    vmem = pl.BlockSpec(memory_space=pltpu.VMEM)
    hbm = pl.BlockSpec(memory_space=pl.ANY)
    smem = pl.BlockSpec(memory_space=pltpu.SMEM)
    dma = pltpu.SemaphoreType.DMA
    channels = latent.shape[1] // 2
    return pl.pallas_call(
        finish_kernel,
        out_shape=[
            jax.ShapeDtypeStruct((ROWS, channels), f32),
            jax.ShapeDtypeStruct((ROWS, channels), f32),
            jax.ShapeDtypeStruct(position.shape, bf16),
        ],
        in_specs=[vmem, vmem, vmem, hbm, vmem, vmem, vmem, vmem, smem, smem],
        out_specs=[vmem, vmem, vmem],
        scratch_shapes=[
            pltpu.VMEM((8, 4, FIRST, 128), bf16),
            pltpu.VMEM((ROWS, whole_out.shape[0]), bf16),
            pltpu.VMEM(whole_out.shape, bf16),
            pltpu.VMEM((2, ROWS, 2 * channels), f32),
            dma((1,)), dma((1,)),
            dma((32,)), dma((32,)),
            dma((1,)), dma((1,)),
        ],
        compiler_params=pltpu.CompilerParams(
            collective_id=1, has_side_effects=True, vmem_limit_bytes=40 << 20
        ),
        name="finish",
    )(o, hidden, modulation, whole_out, w_final, w_patch, position, latent, timestep, sigma_table)


def body(
    hidden, text_states, modulation, w_qkv, w_text, w_out, qk_gain, w_final, w_patch,
    position, latent, text_len, timestep, sigma_table,
):
    scale = np.array([[np.log2(np.e) * HEAD ** -0.5], [1.0]], np.float32)
    gains = jnp.tile(qk_gain * scale, (1, 2))
    kv, tkv, q = project_heads(hidden, text_states, modulation, w_qkv, w_text, gains)
    whole_out = lax.all_gather(w_out, "uly", axis=0, tiled=True)
    o = attend(text_len, q, kv.reshape(-1, 128), tkv.reshape(-1, 128))
    return tuple(
        finish(o, hidden, modulation, whole_out, w_final, w_patch, position, latent, timestep, sigma_table)
    )


def solution(mesh):
    in_specs = (
        P("cfg", ("blk", "uly"), None),
        P("cfg", "blk", None),
        P("cfg", None, None),
        P(None, None, "uly"),
        P(None, None, "uly"),
        P("uly", None),
        P(),
        P(),
        P(),
        P(("blk", "uly"), "cfg"),
        P(("blk", "uly"), None),
        P("cfg"),
        P(),
        P(),
    )
    out_specs = (P(("blk", "uly"), "cfg"), P(("blk", "uly"), "cfg"), P(("blk", "uly"), "cfg"))
    return jax.shard_map(body, mesh=mesh, in_specs=in_specs, out_specs=out_specs, check_vma=False)
```

time: 561 us -> 283 us (0.50)
  waiting for transfers between devices: 313 us -> 116 us
  Pallas kernels: 0 us -> 135 us
  matrix products: 112 us -> 0 us
  local copies, waits for them, and re-layouts: 79.3 us -> 13.6 us
  other arithmetic: 25.1 us -> 0.75 us
  starting transfers between devices: 12.4 us -> 0.04 us
    all_gather x4 -> x0, waiting for transfers between devices: 287 us -> none  [the longest x1 88.4 us: body(): value_rows = lax.all_gather(projected[2], 'blk', axis=0, tiled=True)]
    pallas_call x0 -> x3, Pallas kernels: none -> 135 us  [the longest x1 71.9 us: project_heads(): pl.pallas_call(project_kernel, out_shape=[jax.ShapeDtypeStruct((16, 4, PA...]
    dot_general x42 -> x0, matrix products: 112 us -> none  [the longest x16 68.9 us: fold_block(): jnp.einsum('hqk,khd->hqd', block_weights.astype(jnp.bfloat16), value_bloc...]
    all_gather x1, waiting for transfers between devices: 16.2 us -> 116 us  [body(): whole_out = lax.all_gather(w_out, 'uly', axis=0, tiled=True)]
    while x48 -> x0, local copies, waits for them, and re-layouts: 42.6 us -> none
    dynamic_slice x49 -> x0, local copies, waits for them, and re-layouts: 25 us -> none  [the longest x48 24.4 us: body(): lax.scan(scan_step, (highest, totals, summed), (key_blocks, value_blocks))]
    reduce_sum x21 -> x0, other arithmetic: 21.4 us -> none  [the longest x16 17.3 us: fold_block(): new_total = run_total * shrink + jnp.sum(block_weights, axis=-1)]
    all_to_all x1 -> x0, starting transfers between devices: 11.2 us -> none  [body(): lax.all_to_all(attended, 'uly', split_axis=0, concat_axis=1, tiled=True)]
  transfers between devices with their start and end apart: 7 -> 1, of which waited for: 6 -> 1; matrix products, arithmetic and copies ran while one was open for 29% -> 1% of each run, Pallas kernels for 0% -> 39%
where the time goes in v1:
time: 283 us; the launch traced here: 281 us
  Pallas kernels  135 us (48%)
  waiting for transfers between devices  116 us (41%)
  between operations  15.4 us (5%)
  local copies, waits for them, and re-layouts  13.6 us (5%)
    all_gather x1, waiting for transfers between devices, body(): whole_out = lax.all_gather(w_out, 'uly', axis=0, tiled=True)  116 us
    pallas_call x1, Pallas kernels, project_heads(): pl.pallas_call(project_kernel, out_shape=[jax.ShapeDtypeStruct((16, 4, PA...  71.9 us
    pallas_call x1, Pallas kernels, attend(): pl.pallas_call(attend_kernel, grid=(4,), in_specs=[pl.BlockSpec(memory_sp...  38.1 us
    pallas_call x1, Pallas kernels, finish(): pl.pallas_call(finish_kernel, out_shape=[jax.ShapeDtypeStruct((ROWS, chan...  24.7 us
    unnamed x20, local copies, waits for them, and re-layouts  12.1 us
  transfers between devices with their start and end apart: 1, of which 1 were waited for; matrix products, arithmetic and copies ran while one was open for 1% of the time, Pallas kernels for 39%

profile of v1, /device:TPU:3, one launch (start us, length us, event | category | flops | bytes accessed | tf_op | source)
XLA Modules:
  0.0 280.7 jit_solution(5664497360854799351)
XLA Ops:
  7.2 0.0 copy-start.3
  7.2 0.0 all-gather.2.cloned.1.call-start
  7.2 0.7 all-gather.2.cloned.1.call-update
  7.9 0.8 copy.18.mod_ref
  8.7 0.8 broadcast_multiply_fusion
  9.5 0.1 tile.10.gain_ref
  10.2 1.3 copy.20.wfinal_ref
  11.5 0.8 copy.21.lat_ref
  13.0 0.0 copy-start.1
  13.0 2.0 copy-done.1
  15.1 1.7 copy-done.2
  16.8 0.9 copy-done.6
  17.7 71.9 %project_heads.1 = (bf16[16,4,160,128]{3,2,1,0:T(8,128)(2,1)S(1)}, bf16[16,32,128]{2,1,0:T(8,128)(2,1)S(1)}, bf16[4,4,80,128]{3,2,1,0:T(8,128)(2,1)S(1)}) custom-call(bf16[1,80,2432]{2,1,0:T(8,128)(2,1)S(1)} %copy-done.3, bf16[1,21,2432]{2,1,0:T(8,128)(2,1)S(1)} %copy-done.6, f32[1,5,2432]{2,1,0:T(8,128)S(1)} %copy.18.mod_ref, ...), custom_call_target="tpu_custom_call" | custom-call | tf_op jit(solution)/shard_map/project_heads/pallas_call | solution.py:290
  89.6 0.0 copy-start.4
  89.6 0.0 copy-start.5
  89.6 0.0 copy-start.7
  89.7 38.1 %attend.1.o_ref = bf16[4,8,48,128]{3,2,1,0:T(8,128)(2,1)S(1)} custom-call(s32[1]{0:T(128)S(6)} %copy.25.len_ref, bf16[4,4,80,128]{3,2,1,0:T(8,128)(2,1)S(1)} %get-tuple-element.6.q_ref, bf16[10240,128]{1,0:T(8,128)(2,1)S(1)} %bitcast.2, bf16[512,128]{1,0:T(8,128)(2,1)S(1)} %bitcast.3), custom_call_target="tpu_custom_call" | custom-call | flops 14092861440 | bytes 7864320 | tf_op jit(solution)/shard_map/attend/pallas_call | solution.py:390
  127.7 115.6 %all-gather.2.cloned.1.call-done.wout_ref = bf16[2048,2432]{1,0:T(8,128)(2,1)} async-done(((bf16[256,2432]{1,0:T(8,128)(2,1)}), bf16[2048,2432]{1,0:T(8,128)(2,1)}) %all-gather.2.cloned.1.call-update) | async-done | bytes 9961488 | tf_op jit(solution)/shard_map/all_gather | solution.py:541
  243.3 0.0 copy-done.4
  243.3 3.8 %copy-done = bf16[2048,2432]{1,0:T(8,128)(2,1)S(1)} copy-done((bf16[2048,2432]{1,0:T(8,128)(2,1)S(1)}, bf16[2048,2432]{1,0:T(8,128)(2,1)}, u32[]{:S(2)}) %copy-start) | copy-done | bytes 9961496
  247.2 24.7 %finish.1 = (f32[80,32]{1,0:T(8,128)S(1)}, f32[80,32]{1,0:T(8,128)S(1)}, bf16[80,1216]{1,0:T(8,128)(2,1)S(1)}) custom-call(bf16[4,8,48,128]{3,2,1,0:T(8,128)(2,1)S(1)} %attend.1.o_ref, bf16[1,80,2432]{2,1,0:T(8,128)(2,1)S(1)} %copy-done.3, f32[1,5,2432]{2,1,0:T(8,128)S(1)} %copy.18.mod_ref, bf16[2048,2432]{1,0:T(8,128)(2,1)S(1)} %copy-done, ...), custom_call_target="tpu_custom_call" | custom-call | tf_op jit(solution)/shard_map/finish/pallas_call | solution.py:509
  271.9 0.7 copy.22
  272.5 0.7 copy.23
  273.2 0.7 copy.27
  (7 shorter events, 0.0 us)
Async XLA Ops:
  7.2 5.9 %copy-start.3 = (bf16[1,80,2432]{2,1,0:T(8,128)(2,1)S(1)}, bf16[1,80,2432]{2,1,0:T(8,128)(2,1)}, u32[]{:S(2)}) copy-start(bf16[1,80,2432]{2,1,0:T(8,128)(2,1)} %hid_ref.3) | copy-start | bytes 1167364
  7.2 236.2 %all-gather.2.cloned.1.call-start = ((), (), s32[]{:S(2)}) async-start(), calls=%async_computation | async-start | bytes 11206656 | tf_op jit(solution)/shard_map/all_gather | solution.py:541
  13.0 2.1 copy-start.1
  15.1 1.7 copy-start.2
  16.8 0.9 copy-start.6
  89.6 153.7 %copy-start.4 = (bf16[64,2432]{1,0:T(8,128)(2,1)S(1)}, bf16[64,2432]{1,0:T(8,128)(2,1)}, u32[]{:S(2)}) copy-start(bf16[64,2432]{1,0:T(8,128)(2,1)} %wpatch_ref.1) | copy-start | bytes 933892
  89.6 153.7 %copy-start.5 = (bf16[80,1216]{1,0:T(8,128)(2,1)S(1)}, bf16[80,1216]{1,0:T(8,128)(2,1)}, u32[]{:S(2)}) copy-start(bf16[80,1216]{1,0:T(8,128)(2,1)} %pos_ref.1) | copy-start | bytes 583684
  89.6 153.7 %copy-start.7 = (s32[29]{0:T(128)S(1)}, s32[29]{0:T(128)}, u32[]{:S(2)}) copy-start(s32[29]{0:T(128)} %sigma_ref.1) | copy-start | bytes 352
  243.3 3.8 %copy-start = (bf16[2048,2432]{1,0:T(8,128)(2,1)S(1)}, bf16[2048,2432]{1,0:T(8,128)(2,1)}, u32[]{:S(2)}) copy-start(bf16[2048,2432]{1,0:T(8,128)(2,1)} %all-gather.2.cloned.1.call-done.wout_ref) | copy-start | bytes 29884420
Sparse Core Ops, SparseCore 0:
  9.8 233.4 all-gather.1

commit v2 on v1

--- a/solution.py
+++ b/solution.py
@@ -61,11 +61,11 @@
 
 
 def project_kernel(
-    hid_ref, txt_ref, mod_ref, wqkv_ref, wtext_ref, gain_ref,
-    kv_ref, tkv_ref, q_ref,
+    hid_ref, txt_ref, mod_ref, wqkv_ref, wtext_ref, wout_ref, gain_ref,
+    kv_ref, tkv_ref, q_ref, wx_ref,
     mods, wq, wt, txt, kvst, qst, tst,
     wsem, lsem, bsend, brecv, zsend, zrecv, qsend, qrecv, ysend, yrecv,
-    tzsend, tzrecv, tysend, tyrecv,
+    tzsend, tzrecv, tysend, tyrecv, osend, orecv,
 ):
     c, zh, y, x, zl = coords()
     u = x * 2 + zl
@@ -90,12 +90,12 @@
         w.start()
 
     barrier = pltpu.get_barrier_semaphore()
-    peers = [partner, up, down] + [at(zh_=d) for d in (1, 2, 3)] + [at(y_=d) for d in (1, 2, 3)]
+    peers = [partner, up, down, at(x_=2)] + [at(zh_=d) for d in (1, 2, 3)] + [at(y_=d) for d in (1, 2, 3)]
     for peer in peers:
         pl.semaphore_signal(barrier, inc=1, device_id=peer, device_id_type=MESH)
 
     states = hid_ref[0].astype(f32)
-    modulated = layer_norm(states) * (1.0 + mod_ref[0, 1:2, :]) + mod_ref[0, 0:1, :]
+    modulated = layer_norm(states) * (1.0 + mod_ref[1]) + mod_ref[0]
     mods[u] = modulated.astype(bf16)
     txt[...] = jnp.zeros_like(txt)
     txt[0:TXT_ROWS, :] = txt_ref[0]
@@ -141,8 +141,20 @@
     for i in (0, 1, 2):
         sends[i].start()
 
-    gain_q = gain_ref[0:1, :]
+    gain_q = gain_ref[0:1, :] * float(np.log2(np.e) * HEAD ** -0.5)
     gain_k = gain_ref[1:2, :]
+    gain_q = jnp.concatenate([gain_q, gain_q], axis=1)
+    gain_k = jnp.concatenate([gain_k, gain_k], axis=1)
+    own_half = wout_ref.at[pl.ds(pl.multiple_of(c * 128, 128), 128)]
+    own_out = pltpu.make_async_copy(own_half, wx_ref.at[x], lsem.at[9])
+    own_out.start()
+
+    def out_x(d):
+        return remote(own_half, wx_ref.at[x], osend.at[d - 1], orecv.at[d - 1], at(x_=d))
+
+    def out_x_landed(d):
+        slot = wx_ref.at[lax.rem(x + 4 - d, 4)]
+        return remote(slot, slot, osend.at[d - 1], orecv.at[d - 1], at(x_=d))
 
     def copy_kv(t, p, d):
         h = lax.rem(zh + d, 4)
@@ -254,6 +266,8 @@
     pass_on(0, 0)
     for i in (5, 6, 7, 8):
         arrive[i].wait_recv()
+    for d in (1, 3, 2):
+        out_x(d).start()
     project(3, 2)
     pass_on(1, 3)
     pass_on(2, 1)
@@ -262,6 +276,10 @@
     for i in range(9):
         sends[i].wait_send()
     local_text.wait()
+    own_out.wait()
+    for d in (1, 2, 3):
+        out_x(d).wait_send()
+        out_x_landed(d).wait_recv()
     for d in (1, 2, 3):
         text_z(d).wait_send()
     for d in range(4):
@@ -282,7 +300,7 @@
                 landed_y(t, p, d, e).wait_recv()
 
 
-def project_heads(hidden, text_states, modulation, w_qkv, w_text, gains):
+def project_heads(hidden, text_states, modulation, w_qkv, w_text, w_out, qk_gain):
     width = hidden.shape[2]
     vmem = pl.BlockSpec(memory_space=pltpu.VMEM)
     hbm = pl.BlockSpec(memory_space=pl.ANY)
@@ -293,9 +311,10 @@
             jax.ShapeDtypeStruct((16, 4, PAIR, 128), bf16),
             jax.ShapeDtypeStruct((16, TXT_PAD, 128), bf16),
             jax.ShapeDtypeStruct((4, 4, ROWS, 128), bf16),
+            jax.ShapeDtypeStruct((4, 128, width), bf16),
         ],
-        in_specs=[vmem, vmem, vmem, hbm, hbm, vmem],
-        out_specs=[hbm, hbm, hbm],
+        in_specs=[vmem, vmem, vmem, hbm, hbm, hbm, vmem],
+        out_specs=[hbm, hbm, hbm, hbm],
         scratch_shapes=[
             pltpu.VMEM((8, ROWS, width), bf16),
             pltpu.VMEM((3, width, 256), bf16),
@@ -305,26 +324,96 @@
             pltpu.VMEM((4, 4, ROWS, 128), bf16),
             pltpu.VMEM((4, TXT_PAD, 128), bf16),
             dma((5,)),
-            dma((9,)),
+            dma((10,)),
             dma((9,)), dma((9,)),
             dma((4, 3)), dma((4, 3)),
             dma((4, 3)), dma((4, 3)),
             dma((4, 4, 3)), dma((4, 4, 3)),
             dma((3,)), dma((3,)),
             dma((4, 3)), dma((4, 3)),
+            dma((3,)), dma((3,)),
         ],
         compiler_params=pltpu.CompilerParams(
-            collective_id=0, has_side_effects=True, vmem_limit_bytes=40 << 20
+            collective_id=0, has_side_effects=True, vmem_limit_bytes=56 << 20
         ),
         name="project_heads",
-    )(hidden, text_states, modulation, w_qkv, w_text, gains)
+    )(hidden, text_states, modulation, w_qkv, w_text, w_out, qk_gain)
 
 
 KEYS = 2560
 
 
-def attend_kernel(len_ref, q_ref, kv_ref, tkv_ref, o_ref, q2, v1):
+def attend_kernel(
+    len_ref, q_ref, kv_ref, tkv_ref, wx_ref, o_ref, w_ref,
+    q2, v1, lsem, csend, crecv, usend, urecv, dsend, drecv, fsend, frecv,
+):
     step = pl.program_id(0)
+    c, zh, y, x, zl = coords()
+    other = (1 - c, zh * 4 + y, x * 2 + zl)
+    above = (c, lax.rem(zh + zl, 4) * 4 + y, x * 2 + 1 - zl)
+    below = (c, lax.rem(zh + 3 + zl, 4) * 4 + y, x * 2 + 1 - zl)
+
+    def remote(src, dst, send, recv, to):
+        return pltpu.make_async_remote_copy(
+            src_ref=src, dst_ref=dst, send_sem=send, recv_sem=recv,
+            device_id=to, device_id_type=MESH,
+        )
+
+    def own(i):
+        return pltpu.make_async_copy(wx_ref.at[i], w_ref.at[i, zl, c], lsem.at[i])
+
+    def across(i):
+        return remote(wx_ref.at[i], w_ref.at[i, zl, c], csend.at[i], crecv.at[i], other)
+
+    def across_landed(i):
+        slot = w_ref.at[i, zl, 1 - c]
+        return remote(slot, slot, csend.at[i], crecv.at[i], other)
+
+    def upwards(i):
+        rows = pl.ds(0, 64)
+        return remote(wx_ref.at[i, rows], w_ref.at[i, zl, c, rows], usend.at[i], urecv.at[i], above)
+
+    def downwards(i):
+        rows = pl.ds(64, 64)
+        return remote(wx_ref.at[i, rows], w_ref.at[i, zl, c, rows], dsend.at[i], drecv.at[i], below)
+
+    def from_below(i):
+        slot = w_ref.at[i, 1 - zl, c, pl.ds(0, 64)]
+        return remote(slot, slot, usend.at[i], urecv.at[i], above)
+
+    def from_above(i):
+        slot = w_ref.at[i, 1 - zl, c, pl.ds(64, 64)]
+        return remote(slot, slot, dsend.at[i], drecv.at[i], below)
+
+    def across_later(i):
+        slot = w_ref.at[i, 1 - zl, c]
+        return remote(slot, slot, fsend.at[i], frecv.at[i], other)
+
+    def across_later_landed(i):
+        slot = w_ref.at[i, 1 - zl, 1 - c]
+        return remote(slot, slot, fsend.at[i], frecv.at[i], other)
+
+    @pl.when(step == 0)
+    def _():
+        barrier = pltpu.get_barrier_semaphore()
+        for peer in (other, above, below):
+            pl.semaphore_signal(barrier, inc=1, device_id=peer, device_id_type=MESH)
+        pl.semaphore_wait(barrier, 3)
+        for i in range(4):
+            upwards(i).start()
+            downwards(i).start()
+            across(i).start()
+            own(i).start()
+
+    for late in (2, 3):
+
+        @pl.when(step == late)
+        def _():
+            for i in (2 * late - 4, 2 * late - 3):
+                from_below(i).wait_recv()
+                from_above(i).wait_recv()
+                across_later(i).start()
+
     image = kv_ref.shape[0]
     text = tkv_ref.shape[0]
 
@@ -384,8 +473,20 @@
             high[ROWS * (s + 1) - FIRST : ROWS * (s + 1)],
         ).astype(bf16)
 
-
-def attend(text_len, q, kv, tkv):
+    @pl.when(step == 3)
+    def _():
+        for i in range(4):
+            own(i).wait()
+            across(i).wait_send()
+            across_landed(i).wait_recv()
+            upwards(i).wait_send()
+            downwards(i).wait_send()
+            across_later(i).wait_send()
+            across_later_landed(i).wait_recv()
+
+
+def attend(text_len, q, kv, tkv, wx):
+    dma = pltpu.SemaphoreType.DMA
     image, text = kv.shape[0], tkv.shape[0]
     return pl.pallas_call(
         attend_kernel,
@@ -395,21 +496,31 @@
             pl.BlockSpec((1, 4, ROWS, 128), lambda i: (i, 0, 0, 0)),
             pl.BlockSpec((image, 128), lambda i: (0, 0)),
             pl.BlockSpec((text, 128), lambda i: (0, 0)),
+            pl.BlockSpec(memory_space=pl.ANY),
         ],
-        out_specs=pl.BlockSpec((1, 8, FIRST, 128), lambda i: (i, 0, 0, 0)),
-        out_shape=jax.ShapeDtypeStruct((4, 8, FIRST, 128), bf16),
+        out_specs=[
+            pl.BlockSpec((1, 8, FIRST, 128), lambda i: (i, 0, 0, 0)),
+            pl.BlockSpec(memory_space=pl.ANY),
+        ],
+        out_shape=[
+            jax.ShapeDtypeStruct((4, 8, FIRST, 128), bf16),
+            jax.ShapeDtypeStruct((4, 2, 2) + wx.shape[1:], bf16),
+        ],
         scratch_shapes=[
             pltpu.VMEM((4 * PAIR, 128), bf16),
             pltpu.VMEM((image + text, 128), bf16),
-        ],
-        compiler_params=pltpu.CompilerParams(vmem_limit_bytes=44 << 20),
+        ]
+        + [dma((4,))] * 9,
+        compiler_params=pltpu.CompilerParams(
+            collective_id=2, has_side_effects=True, vmem_limit_bytes=44 << 20
+        ),
         cost_estimate=pl.CostEstimate(
             flops=4 * 4 * 4 * PAIR * (image + text) * 128,
             bytes_accessed=3 * image * 128 * 2,
             transcendentals=4 * 4 * PAIR * (image + text),
         ),
         name="attend",
-    )(text_len, q, kv, tkv)
+    )(text_len, q, kv, tkv, wx)
 
 
 def finish_kernel(
@@ -479,9 +590,11 @@
             att[FIRST:ROWS, columns] = rest[2 * FIRST - ROWS : FIRST]
     load.wait()
     projected = jnp.dot(att[...], wo[...], preferred_element_type=f32)
-    mixed = states + mod_ref[0, 2:3, :] * projected
-    final = (layer_norm(mixed) * (1.0 + mod_ref[0, 4:5, :]) + mod_ref[0, 3:4, :]).astype(bf16)
-    velocity = jnp.dot(final, wfinal_ref[...], preferred_element_type=f32)
+    mixed = states + mod_ref[2] * projected
+    final = (layer_norm(mixed) * (1.0 + mod_ref[4]) + mod_ref[3]).astype(bf16)
+    velocity = lax.dot_general(
+        wfinal_ref[...], final, (((1,), (1,)), ((), ())), preferred_element_type=f32
+    )
     vel[0] = velocity
     exchange = remote(vel.at[0], vel.at[1], vsend.at[0], vrecv.at[0], other)
     exchange.start()
@@ -491,11 +604,11 @@
     uncond = jnp.where(is_cond, partner, velocity)
     guided = uncond + guidance * (cond - uncond)
     latent = lat_ref[...] + (sigma_next - sigma_now) * guided
-    embedded = jnp.dot(latent.astype(bf16), patch, preferred_element_type=f32)
+    embedded = jnp.dot(latent.T.astype(bf16), patch, preferred_element_type=f32)
     next_ref[...] = (embedded + pos_ref[...].astype(f32)).astype(bf16)
-    channels = guided_ref.shape[1]
-    guided_ref[...] = jnp.where(is_cond, guided[:, 0:channels], guided[:, channels:])
-    latent_ref[...] = jnp.where(is_cond, latent[:, 0:channels], latent[:, channels:])
+    channels = guided_ref.shape[0]
+    guided_ref[...] = jnp.where(is_cond, guided[0:channels], guided[channels:])
+    latent_ref[...] = jnp.where(is_cond, latent[0:channels], latent[channels:])
     for k in range(1, 32):
         out_copy(k).wait_send()
 
@@ -505,12 +618,12 @@
     hbm = pl.BlockSpec(memory_space=pl.ANY)
     smem = pl.BlockSpec(memory_space=pltpu.SMEM)
     dma = pltpu.SemaphoreType.DMA
-    channels = latent.shape[1] // 2
+    channels = latent.shape[0] // 2
     return pl.pallas_call(
         finish_kernel,
         out_shape=[
-            jax.ShapeDtypeStruct((ROWS, channels), f32),
-            jax.ShapeDtypeStruct((ROWS, channels), f32),
+            jax.ShapeDtypeStruct((channels, ROWS), f32),
+            jax.ShapeDtypeStruct((channels, ROWS), f32),
             jax.ShapeDtypeStruct(position.shape, bf16),
         ],
         in_specs=[vmem, vmem, vmem, hbm, vmem, vmem, vmem, vmem, smem, smem],
@@ -519,7 +632,7 @@
             pltpu.VMEM((8, 4, FIRST, 128), bf16),
             pltpu.VMEM((ROWS, whole_out.shape[0]), bf16),
             pltpu.VMEM(whole_out.shape, bf16),
-            pltpu.VMEM((2, ROWS, 2 * channels), f32),
+            pltpu.VMEM((2, 2 * channels, ROWS), f32),
             dma((1,)), dma((1,)),
             dma((32,)), dma((32,)),
             dma((1,)), dma((1,)),
@@ -535,14 +648,14 @@
     hidden, text_states, modulation, w_qkv, w_text, w_out, qk_gain, w_final, w_patch,
     position, latent, text_len, timestep, sigma_table,
 ):
-    scale = np.array([[np.log2(np.e) * HEAD ** -0.5], [1.0]], np.float32)
-    gains = jnp.tile(qk_gain * scale, (1, 2))
-    kv, tkv, q = project_heads(hidden, text_states, modulation, w_qkv, w_text, gains)
-    whole_out = lax.all_gather(w_out, "uly", axis=0, tiled=True)
-    o = attend(text_len, q, kv.reshape(-1, 128), tkv.reshape(-1, 128))
-    return tuple(
-        finish(o, hidden, modulation, whole_out, w_final, w_patch, position, latent, timestep, sigma_table)
+    modulation = jnp.swapaxes(modulation, 0, 1)
+    kv, tkv, q, wx = project_heads(hidden, text_states, modulation, w_qkv, w_text, w_out, qk_gain)
+    o, whole_out = attend(text_len, q, kv.reshape(-1, 128), tkv.reshape(-1, 128), wx)
+    guided, next_latent, next_hidden = finish(
+        o, hidden, modulation, whole_out.reshape(-1, w_out.shape[1]), w_final.T, w_patch,
+        position, latent.T, timestep, sigma_table,
     )
+    return guided.T, next_latent.T, next_hidden
 
 
 def solution(mesh):

time: 283 us -> 144 us (0.51)
  waiting for transfers between devices: 116 us -> 0 us
  between operations: 15.4 us -> 2.05 us
  Pallas kernels: 135 us -> 130 us
    all_gather x1 -> x0, waiting for transfers between devices: 116 us -> none  [body(): whole_out = lax.all_gather(w_out, 'uly', axis=0, tiled=True)]
    pallas_call x1, Pallas kernels: 71.9 us -> 65.2 us  [project_heads(): pl.pallas_call(project_kernel, out_shape=[jax.ShapeDtypeStruct((16, 4, PA...]
    pallas_call x1, Pallas kernels: 38.1 us -> 42.1 us  [attend(): pl.pallas_call(attend_kernel, grid=(4,), in_specs=[pl.BlockSpec(memory_sp...]
    unnamed x20 -> x27, local copies, waits for them, and re-layouts: 12.1 us -> 11.1 us
  transfers between devices with their start and end apart: 1 -> 0, of which waited for: 1 -> 0; matrix products, arithmetic and copies ran while one was open for 1% -> 0% of each run, Pallas kernels for 39% -> 0%
where the time goes in v2:
time: 144 us; the launch traced here: 143 us
  Pallas kernels  130 us (90%)
  local copies, waits for them, and re-layouts  11.1 us (8%)
  between operations  2.05 us (1%)
    pallas_call x1, Pallas kernels, project_heads(): pl.pallas_call(project_kernel, out_shape=[jax.ShapeDtypeStruct((16, 4, PA...  65.2 us
    pallas_call x1, Pallas kernels, attend(): pl.pallas_call(attend_kernel, grid=(4,), in_specs=[pl.BlockSpec(memory_sp...  42.1 us
    pallas_call x1, Pallas kernels, finish(): pl.pallas_call(finish_kernel, out_shape=[jax.ShapeDtypeStruct((channels,...  22.4 us
    unnamed x27, local copies, waits for them, and re-layouts  11.1 us

profile of v2, /device:TPU:3, one launch (start us, length us, event | category | flops | bytes accessed | tf_op | source)
XLA Modules:
  0.0 142.8 jit_solution(15595328837404288936)
XLA Ops:
  0.6 65.2 %project_heads.1 = (bf16[16,4,160,128]{3,2,1,0:T(8,128)(2,1)}, bf16[16,32,128]{2,1,0:T(8,128)(2,1)}, bf16[4,4,80,128]{3,2,1,0:T(8,128)(2,1)}, bf16[4,128,2432]{2,1,0:T(8,128)(2,1)}) custom-call(bf16[1,80,2432]{2,1,0:T(8,128)(2,1)} %hid_ref.3, bf16[1,21,2432]{2,1,0:T(8,128)(2,1)} %txt_ref.1, f32[5,1,2432]{2,1,0:T(1,128)} %bitcast.10, ...), custom_call_target="tpu_custom_call" | custom-call | tf_op jit(solution)/shard_map/project_heads/pallas_call | solution.py:308
  66.5 0.0 copy-start.8
  66.5 1.7 %copy-done.8 = bf16[16,4,160,128]{3,2,1,0:T(8,128)(2,1)S(1)} copy-done((bf16[16,4,160,128]{3,2,1,0:T(8,128)(2,1)S(1)}, bf16[16,4,160,128]{3,2,1,0:T(8,128)(2,1)}, u32[]{:S(2)}) %copy-start.8) | copy-done | bytes 2621464
  68.2 1.7 %copy-done.9 = bf16[4,128,2432]{2,1,0:T(8,128)(2,1)S(1)} copy-done((bf16[4,128,2432]{2,1,0:T(8,128)(2,1)S(1)}, bf16[4,128,2432]{2,1,0:T(8,128)(2,1)}, u32[]{:S(2)}) %copy-start.9) | copy-done | bytes 2490392
  69.9 0.0 copy-start.10
  69.9 1.0 copy-done.10
  70.9 0.9 copy-done.11
  71.8 0.0 copy-start.5
  71.8 0.0 copy-start.6
  71.8 0.0 copy-start.7
  71.8 42.1 %attend.1 = (bf16[4,8,48,128]{3,2,1,0:T(8,128)(2,1)S(1)}, bf16[4,2,2,128,2432]{4,3,2,1,0:T(8,128)(2,1)}) custom-call(s32[1]{0:T(128)S(6)} %copy.20.len_ref, bf16[4,4,80,128]{3,2,1,0:T(8,128)(2,1)S(1)} %copy-done.10, bf16[10240,128]{1,0:T(8,128)(2,1)S(1)} %bitcast.15, bf16[512,128]{1,0:T(8,128)(2,1)S(1)} %bitcast.16, bf16[4,128,2432]{2,1,0:T(8,128)(2,1)S(1)} %copy-done.9), custom_call_target="tpu_custom_call" | custom-call | flops 14092861440 | bytes 7864320 | tf_op jit(solution)/shard_map/attend/pallas_call | solution.py:491
  114.6 0.0 copy-done.1
  114.6 0.0 copy-done.2
  114.6 0.0 copy-done.3
  114.6 0.0 copy-done.4
  114.6 0.0 copy-done.5
  114.6 0.0 copy-done.6
  114.6 0.0 copy-done.7
  114.7 0.0 copy-start
  114.7 3.8 %copy-done = bf16[4,2,2,128,2432]{4,3,2,1,0:T(8,128)(2,1)S(1)} copy-done((bf16[4,2,2,128,2432]{4,3,2,1,0:T(8,128)(2,1)S(1)}, bf16[4,2,2,128,2432]{4,3,2,1,0:T(8,128)(2,1)}, u32[]{:S(2)}) %copy-start) | copy-done | bytes 9961496
  118.5 22.4 %finish.1 = (f32[32,80]{1,0:T(8,128)S(1)}, f32[32,80]{1,0:T(8,128)S(1)}, bf16[80,1216]{1,0:T(8,128)(2,1)S(1)}) custom-call(bf16[4,8,48,128]{3,2,1,0:T(8,128)(2,1)S(1)} %get-tuple-element.16.o_ref, bf16[1,80,2432]{2,1,0:T(8,128)(2,1)S(1)} %copy-done.1, f32[5,1,2432]{2,1,0:T(1,128)S(1)} %bitcast.11, bf16[2048,2432]{1,0:T(8,128)(2,1)S(1)} %bitcast.8, ...), custom_call_target="tpu_custom_call" | custom-call | tf_op jit(solution)/shard_map/finish/pallas_call | solution.py:622
  140.9 0.6 copy.22
  141.5 0.6 copy.23
  142.1 0.7 copy.24
  (6 shorter events, 0.0 us)
Async XLA Ops:
  66.5 1.7 %copy-start.8 = (bf16[16,4,160,128]{3,2,1,0:T(8,128)(2,1)S(1)}, bf16[16,4,160,128]{3,2,1,0:T(8,128)(2,1)}, u32[]{:S(2)}) copy-start(bf16[16,4,160,128]{3,2,1,0:T(8,128)(2,1)} %get-tuple-element.13) | copy-start | bytes 7864324
  68.2 1.7 %copy-start.9 = (bf16[4,128,2432]{2,1,0:T(8,128)(2,1)S(1)}, bf16[4,128,2432]{2,1,0:T(8,128)(2,1)}, u32[]{:S(2)}) copy-start(bf16[4,128,2432]{2,1,0:T(8,128)(2,1)} %get-tuple-element.15.wx_ref) | copy-start | bytes 7471108
  69.9 1.0 copy-start.10
  70.9 0.9 copy-start.11
  71.8 42.8 %copy-start.1 = (bf16[1,80,2432]{2,1,0:T(8,128)(2,1)S(1)}, bf16[1,80,2432]{2,1,0:T(8,128)(2,1)}, u32[]{:S(2)}) copy-start(bf16[1,80,2432]{2,1,0:T(8,128)(2,1)} %hid_ref.3) | copy-start | bytes 1167364
  71.8 42.8 %copy-start.2 = (bf16[2432,64]{0,1:T(8,128)(2,1)S(1)}, bf16[2432,64]{0,1:T(8,128)(2,1)}, u32[]{:S(2)}) copy-start(bf16[2432,64]{0,1:T(8,128)(2,1)} %param.21) | copy-start | bytes 933892
  71.8 42.8 %copy-start.3 = (bf16[64,2432]{1,0:T(8,128)(2,1)S(1)}, bf16[64,2432]{1,0:T(8,128)(2,1)}, u32[]{:S(2)}) copy-start(bf16[64,2432]{1,0:T(8,128)(2,1)} %wpatch_ref.1) | copy-start | bytes 933892
  71.8 42.8 %copy-start.4 = (bf16[80,1216]{1,0:T(8,128)(2,1)S(1)}, bf16[80,1216]{1,0:T(8,128)(2,1)}, u32[]{:S(2)}) copy-start(bf16[80,1216]{1,0:T(8,128)(2,1)} %pos_ref.1) | copy-start | bytes 583684
  71.8 42.8 %copy-start.5 = (f32[1,5,2432]{2,0,1:T(1,128)S(1)}, f32[1,5,2432]{2,0,1:T(1,128)}, u32[]{:S(2)}) copy-start(f32[1,5,2432]{2,0,1:T(1,128)} %param.16) | copy-start | bytes 145924
  71.8 42.8 %copy-start.6 = (f32[80,64]{0,1:T(8,128)S(1)}, f32[80,64]{0,1:T(8,128)}, u32[]{:S(2)}) copy-start(f32[80,64]{0,1:T(8,128)} %param.24) | copy-start | bytes 61444
  71.8 42.8 %copy-start.7 = (s32[29]{0:T(128)S(1)}, s32[29]{0:T(128)}, u32[]{:S(2)}) copy-start(s32[29]{0:T(128)} %sigma_ref.1) | copy-start | bytes 352
  114.7 3.8 %copy-start = (bf16[4,2,2,128,2432]{4,3,2,1,0:T(8,128)(2,1)S(1)}, bf16[4,2,2,128,2432]{4,3,2,1,0:T(8,128)(2,1)}, u32[]{:S(2)}) copy-start(bf16[4,2,2,128,2432]{4,3,2,1,0:T(8,128)(2,1)} %get-tuple-element.17) | copy-start | bytes 29884420

commit v3 on v0

v3 whole, which is shorter than its diff:
```python
import jax
import jax.numpy as jnp
import numpy as np
from jax import lax
from jax.experimental import pallas as pl
from jax.experimental.pallas import tpu as pltpu
from jax.sharding import PartitionSpec as P

HEAD = 64
guidance = 3.5
epsilon = 1e-06
MESH = pl.DeviceIdType.MESH
bf16 = jnp.bfloat16
f32 = jnp.float32

ROWS = 80
PAIR = 160
TXT_ROWS = 21
TXT_PAD = 32
TXT_KEYS = 16 * TXT_PAD
KEYS = 16 * PAIR
QUERIES = 4 * PAIR
FIRST = 48
OUT_HALF = 128
STAGES = (0, 3, 1, 2)


def layer_norm(values):
    average = jnp.mean(values, axis=-1, keepdims=True)
    centered = values - average
    spread = jnp.mean(centered * centered, axis=-1, keepdims=True)
    return centered * lax.rsqrt(spread + epsilon)


def low_lanes(rows):
    return lax.broadcasted_iota(jnp.int32, (rows, 128), 1) < HEAD


def head_norm(values, gain):
    low = low_lanes(values.shape[0])
    columns = []
    for t in range(2):
        x = values[:, 128 * t : 128 * t + 128]
        sq = x * x
        a = jnp.sum(jnp.where(low, sq, 0.0), axis=1, keepdims=True)
        b = jnp.sum(jnp.where(low, 0.0, sq), axis=1, keepdims=True)
        scale = lax.rsqrt(jnp.where(low, a, b) * (1.0 / HEAD) + epsilon)
        columns.append(x * scale * gain)
    return columns


def pack_heads(left, right):
    low = low_lanes(left[0].shape[0])
    out = []
    for t in range(2):
        out.append(jnp.where(low, left[t], pltpu.roll(right[t], HEAD, 1)))
        out.append(jnp.where(low, pltpu.roll(left[t], HEAD, 1), right[t]))
    return out


def values_and_ones(block):
    wide = block.astype(f32)
    return jnp.where(low_lanes(wide.shape[0]), pltpu.roll(wide, HEAD, 1), 1.0).astype(bf16)


def kernel(
    hid_ref, txt_ref, mod_ref, wqkv_ref, wtext_ref, wout_ref, gain_ref, wfinal_ref, wpatch_ref,
    pos_ref, lat_ref, len_ref, time_ref, sigma_ref,
    guided_ref, latent_ref, next_ref,
    mods, wq, wt, txt, kvst, qst, tst, kvb, v1, qb, q2, tkv, tv1, top, acc, ob, got, att, wo, vel,
    wsem, lsem, bsend, brecv, zsend, zrecv, qsend, qrecv, ysend, yrecv,
    tzsend, tzrecv, tysend, tyrecv, xsend, xrecv, usend, urecv, dsend, drecv,
    csend, crecv, fsend, frecv, osend, orecv, vsend, vrecv,
):
    c = lax.axis_index("cfg")
    b = lax.axis_index("blk")
    u = lax.axis_index("uly")
    zh, y, x, zl = b // 4, b % 4, u // 2, u % 2

    def at(dz=0, dy=0, dx=0, dl=0):
        return (
            c,
            lax.rem(zh + dz, 4) * 4 + lax.rem(y + dy, 4),
            lax.rem(x + dx, 4) * 2 + lax.rem(zl + dl, 2),
        )

    other = (1 - c, b, u)
    partner, up, down = at(dl=1), at(dx=1), at(dx=3)
    above = (c, lax.rem(zh + zl, 4) * 4 + y, x * 2 + 1 - zl)
    below = (c, lax.rem(zh + 3 + zl, 4) * 4 + y, x * 2 + 1 - zl)

    qkv_in = [pltpu.make_async_copy(wqkv_ref.at[i], wq.at[i], wsem.at[i]) for i in range(3)]
    text_in = [pltpu.make_async_copy(wtext_ref.at[i], wt.at[i], wsem.at[3 + i]) for i in range(2)]
    out_in = [
        pltpu.make_async_copy(
            wout_ref.at[pl.ds(OUT_HALF * i, OUT_HALF)], wo.at[x, zl, i], wsem.at[5 + i]
        )
        for i in range(2)
    ]
    for copy in text_in + qkv_in + out_in:
        copy.start()

    barrier = pltpu.get_barrier_semaphore()
    peers = [at(dz=k // 8, dx=k % 8 // 2, dl=k % 2) for k in range(1, 32)]
    peers += [at(dy=d) for d in (1, 2, 3)] + [other]
    for peer in peers:
        pl.semaphore_signal(barrier, inc=1, device_id=peer, device_id_type=MESH)

    modulated = layer_norm(hid_ref[0].astype(f32)) * (1.0 + mod_ref[1]) + mod_ref[0]
    mods[u] = modulated.astype(bf16)
    txt[...] = jnp.zeros_like(txt)
    txt[0:TXT_ROWS, :] = txt_ref[0]
    pl.semaphore_wait(barrier, len(peers))

    def remote(src, dst, send, recv, to):
        return pltpu.make_async_remote_copy(
            src_ref=src, dst_ref=dst, send_sem=send, recv_sem=recv,
            device_id=to, device_id_type=MESH,
        )


    def shard(i, dx, dl, part, to):
        s = lax.rem(x + dx, 4) * 2 + (zl if dl == 0 else 1 - zl)
        ref = mods.at[s]
        if part == 1:
            ref = mods.at[s, pl.ds(0, FIRST)]
        elif part == 2:
            ref = mods.at[s, pl.ds(FIRST, ROWS - FIRST)]
        return remote(ref, ref, bsend.at[i], brecv.at[i], to)

    sends = [
        shard(0, 0, 0, 0, partner),
        shard(1, 0, 0, 0, up),
        shard(2, 0, 0, 0, down),
        shard(3, 0, 1, 0, up),
        shard(4, 0, 1, 0, down),
        shard(5, 3, 0, 1, up),
        shard(6, 1, 0, 2, down),
        shard(7, 3, 1, 1, up),
        shard(8, 1, 1, 2, down),
    ]
    arrive = [
        shard(0, 0, 1, 0, partner),
        shard(1, 3, 0, 0, up),
        shard(2, 1, 0, 0, down),
        shard(3, 3, 1, 0, up),
        shard(4, 1, 1, 0, down),
        shard(5, 2, 0, 1, up),
        shard(6, 2, 0, 2, down),
        shard(7, 2, 1, 1, up),
        shard(8, 2, 1, 2, down),
    ]
    for i in (0, 1, 2):
        sends[i].start()

    gain_q = gain_ref[0:1, :] * float(np.log2(np.e) * HEAD ** -0.5)
    gain_k = gain_ref[1:2, :]
    gain_q = jnp.concatenate([gain_q, gain_q], axis=1)
    gain_k = jnp.concatenate([gain_k, gain_k], axis=1)


    def source(d):
        return lax.rem(zh + 4 - d, 4) * 4 + y

    def kv_slot(t, block):
        return kvb.at[t, pl.ds(pl.multiple_of(block * PAIR, PAIR), PAIR)]

    def copy_kv(t, d):
        h = lax.rem(zh + d, 4)
        return remote(kvst.at[t, h], kv_slot(t, b), zsend.at[t, d - 1], zrecv.at[t, d - 1], at(dz=d))

    def landed_kv(t, d):
        slot = kv_slot(t, source(d))
        return remote(slot, slot, zsend.at[t, d - 1], zrecv.at[t, d - 1], at(dz=d))

    def copy_q(t, d):
        h = lax.rem(zh + d, 4)
        return remote(qst.at[t, h], qb.at[t, zh], qsend.at[t, d - 1], qrecv.at[t, d - 1], at(dz=d))

    def landed_q(t, d):
        slot = qb.at[t, lax.rem(zh + 4 - d, 4)]
        return remote(slot, slot, qsend.at[t, d - 1], qrecv.at[t, d - 1], at(dz=d))

    def copy_y(t, d, e):
        src = kvst.at[t, zh] if d == 0 else kv_slot(t, source(d))
        dst = kv_slot(t, source(d))
        return remote(src, dst, ysend.at[t, d, e - 1], yrecv.at[t, d, e - 1], at(dy=e))

    def landed_y(t, d, e):
        slot = kv_slot(t, lax.rem(zh + 4 - d, 4) * 4 + lax.rem(y + 4 - e, 4))
        return remote(slot, slot, ysend.at[t, d, e - 1], yrecv.at[t, d, e - 1], at(dy=e))

    def own_kv(t):
        return pltpu.make_async_copy(kvst.at[t, zh], kv_slot(t, b), lsem.at[t])

    def own_q(t):
        return pltpu.make_async_copy(qst.at[t, zh], qb.at[t, zh], lsem.at[4 + t])

    def text_slot(block):
        return tkv.at[pl.ds(pl.multiple_of(block * TXT_PAD, TXT_PAD), TXT_PAD)]

    def text_z(d):
        h = lax.rem(zh + d, 4)
        return remote(tst.at[h], text_slot(b), tzsend.at[d - 1], tzrecv.at[d - 1], at(dz=d))

    def text_z_landed(d):
        slot = text_slot(source(d))
        return remote(slot, slot, tzsend.at[d - 1], tzrecv.at[d - 1], at(dz=d))

    def text_y(d, e):
        src = tst.at[zh] if d == 0 else text_slot(source(d))
        return remote(src, text_slot(source(d)), tysend.at[d, e - 1], tyrecv.at[d, e - 1], at(dy=e))

    def text_y_landed(d, e):
        slot = text_slot(lax.rem(zh + 4 - d, 4) * 4 + lax.rem(y + 4 - e, 4))
        return remote(slot, slot, tysend.at[d, e - 1], tyrecv.at[d, e - 1], at(dy=e))

    own_text = pltpu.make_async_copy(tst.at[zh], text_slot(b), lsem.at[8])


    def out_x(d):
        src = wout_ref.at[pl.ds(pl.multiple_of(c * OUT_HALF, OUT_HALF), OUT_HALF)]
        return remote(src, wo.at[x, zl, c], xsend.at[d - 1], xrecv.at[d - 1], at(dx=d))

    def out_x_landed(d):
        slot = wo.at[lax.rem(x + 4 - d, 4), zl, c]
        return remote(slot, slot, xsend.at[d - 1], xrecv.at[d - 1], at(dx=d))

    half = OUT_HALF // 2

    def out_z(i):
        j = lax.rem(x + i, 4)
        copies = []
        for k, to, send, recv in ((0, above, usend, urecv), (1, below, dsend, drecv)):
            ref = wo.at[j, zl, c, pl.ds(half * k, half)]
            src = ref
            if i == 0:
                src = wout_ref.at[pl.ds(pl.multiple_of(c * OUT_HALF + half * k, half), half)]
            copies.append(remote(src, ref, send.at[i], recv.at[i], to))
        return copies

    def out_z_landed(i):
        j = lax.rem(x + i, 4)
        copies = []
        for k, to, send, recv in ((0, above, usend, urecv), (1, below, dsend, drecv)):
            ref = wo.at[j, 1 - zl, c, pl.ds(half * k, half)]
            copies.append(remote(ref, ref, send.at[i], recv.at[i], to))
        return copies

    def out_core(i, later, landed=False):
        j = lax.rem(x + i, 4)
        slot = wo.at[j, 1 - zl if later else zl, 1 - c if landed else c]
        send, recv = (fsend, frecv) if later else (csend, crecv)
        return remote(slot, slot, send.at[i], recv.at[i], other)

    def start_out_z(i):
        for copy in out_z(i):
            copy.start()

    def pass_out(i):
        for copy in out_z_landed(i):
            copy.wait_recv()
        out_core(i, True).start()


    def back(t, dx, dz, dl):
        src = ob.at[t, lax.rem(zh + dz, 4) * 2 + lax.rem(zl + dl, 2)]
        return remote(src, got.at[u, zh], osend.at[t, dz, dl], orecv.at[t, dz, dl], at(dz=dz, dx=dx, dl=dl))

    def back_landed(t, dx, dz, dl):
        slot = got.at[lax.rem(x + 4 - dx, 4) * 2 + lax.rem(zl + dl, 2), lax.rem(zh + 4 - dz, 4)]
        return remote(slot, slot, osend.at[t, dz, dl], orecv.at[t, dz, dl], at(dz=dz, dx=dx, dl=dl))

    own_back = pltpu.make_async_copy(ob.at[0, zh * 2 + zl], got.at[u, zh], lsem.at[9])

    for copy in text_in:
        copy.wait()
    rows = txt[...]
    tk = head_norm(jnp.dot(rows, wt[0], preferred_element_type=f32), gain_k)
    tv = jnp.dot(rows, wt[1], preferred_element_type=f32)
    for h, value in enumerate(pack_heads(tk, [tv[:, 0:128], tv[:, 128:256]])):
        tst[h] = value.astype(bf16)
    for d in (1, 2, 3):
        text_z(d).start()
    for e in (1, 2, 3):
        text_y(0, e).start()
    own_text.start()
    for copy in qkv_in:
        copy.wait()

    def project(t):
        p = lax.rem(x + STAGES[t], 4)
        pair = mods[pl.ds(p * 2, 2)].reshape(PAIR, mods.shape[2])
        ks = head_norm(jnp.dot(pair, wq[1], preferred_element_type=f32), gain_k)
        vs = jnp.dot(pair, wq[2], preferred_element_type=f32)
        for h, value in enumerate(pack_heads(ks, [vs[:, 0:128], vs[:, 128:256]])):
            kvst[t, h] = value.astype(bf16)
        for d in (2, 1, 3):
            copy_kv(t, d).start()
        for e in (2, 1, 3):
            copy_y(t, 0, e).start()
        own_kv(t).start()
        qs = head_norm(jnp.dot(pair, wq[0], preferred_element_type=f32), gain_q)
        for h, value in enumerate(pack_heads([v[0:ROWS] for v in qs], [v[ROWS:PAIR] for v in qs])):
            qst[t, h] = value.astype(bf16)
        for d in (2, 1, 3):
            copy_q(t, d).start()
        own_q(t).start()

    def pass_on(t):
        for d in (1, 3, 2):
            landed_kv(t, d).wait_recv()
            for e in (2, 1, 3):
                copy_y(t, d, e).start()

    arrive[0].wait_recv()
    sends[3].start()
    sends[4].start()
    arrive[1].wait_recv()
    sends[5].start()
    arrive[2].wait_recv()
    sends[6].start()
    project(0)
    for d in (1, 2, 3):
        text_z_landed(d).wait_recv()
        for e in (1, 2, 3):
            text_y(d, e).start()
    arrive[3].wait_recv()
    sends[7].start()
    arrive[4].wait_recv()
    sends[8].start()
    project(1)
    pass_on(0)
    project(2)
    own_text.wait()
    for d in range(4):
        for e in (1, 2, 3):
            text_y_landed(d, e).wait_recv()
    tv1[...] = values_and_ones(tkv[...])
    for i in (5, 6, 7, 8):
        arrive[i].wait_recv()
    out_x(1).start()
    out_x(3).start()
    project(3)
    pass_on(1)

    def fold(carry, q, keys, values, usable):
        high, total = carry
        scores = lax.dot_general(q, keys, (((1,), (1,)), ((), ())), preferred_element_type=f32)
        if usable is not None:
            scores = jnp.where(usable, scores, -1e30)
        new_high = jnp.maximum(high, jnp.max(scores, axis=1, keepdims=True))
        weights = jnp.exp2(scores - new_high).astype(bf16)
        shrink = jnp.exp2(high - new_high)
        return new_high, total * shrink + jnp.dot(weights, values, preferred_element_type=f32)

    row = lax.broadcasted_iota(jnp.int32, (1, TXT_KEYS), 1)
    block = row // TXT_PAD
    within = row - block * TXT_PAD
    usable = jnp.logical_and(within < TXT_ROWS, block * TXT_ROWS + within < len_ref[0])

    def stage(s, _):
        @pl.when(s == 1)
        def _():
            pass_on(2)
            start_out_z(0)
            out_x(2).start()

        @pl.when(s == 2)
        def _():
            for i in (1, 3):
                out_x_landed(i).wait_recv()
            for i in (1, 3):
                start_out_z(i)
                out_core(i, False).start()

        @pl.when(s == 3)
        def _():
            out_x_landed(2).wait_recv()
            start_out_z(2)
            out_core(2, False).start()

        own_q(s).wait()
        for d in (1, 2, 3):
            landed_q(s, d).wait_recv()
        low = low_lanes(ROWS)
        for p in range(4):
            packed = qb[s, p].astype(f32)
            q2[s, PAIR * p : PAIR * p + ROWS, :] = jnp.where(low, packed, 0.0).astype(bf16)
            q2[s, PAIR * p + ROWS : PAIR * p + PAIR, :] = jnp.where(
                low, pltpu.roll(packed, HEAD, 1), 0.0
            ).astype(bf16)
        first = (jnp.full((QUERIES, 1), -1e30, f32), jnp.zeros((QUERIES, 128), f32))
        top[s], acc[s] = fold(first, q2[s], tkv[...], tv1[...], usable)
        own_kv(s).wait()
        for d in range(4):
            for e in (1, 2, 3):
                landed_y(s, d, e).wait_recv()

        @pl.loop(0, KEYS // 512)
        def _(n):
            rows = pl.ds(pl.multiple_of(n * 512, 512), 512)
            v1[s, rows] = values_and_ones(kvb[s, rows])

        def unit(j, _):
            i = jnp.minimum(j, s)
            k = jnp.where(j < s, s, j - s)
            high, total = fold((top[i], acc[i]), q2[i], kvb[k], v1[k], None)
            top[i] = high
            acc[i] = total

            @pl.when(jnp.logical_and(s == 1, j == 0))
            def _():
                pass_on(3)

            @pl.when(jnp.logical_and(s == 2, j == 3))
            def _():
                pass_out(0)

            @pl.when(jnp.logical_and(s == 3, j == 3))
            def _():
                pass_out(1)
                pass_out(3)

            @pl.when(jnp.logical_and(s == 3, jnp.logical_or(j < 3, j == 6)))
            def _():
                out = acc[i]
                out = out / out[:, HEAD : HEAD + 1]
                turned = pltpu.roll(out, HEAD, 1)
                low = low_lanes(FIRST)
                for n in range(8):
                    ob[i, n] = jnp.where(
                        low,
                        out[ROWS * n : ROWS * n + FIRST],
                        turned[ROWS * (n + 1) - FIRST : ROWS * (n + 1)],
                    ).astype(bf16)
                for t in range(4):

                    @pl.when(i == t)
                    def _():
                        for dz in (2, 1, 3, 0):
                            for dl in range(2):
                                if t + dz + dl == 0:
                                    own_back.start()
                                else:
                                    back(t, STAGES[t], dz, dl).start()

            return 0

        lax.fori_loop(0, 2 * s + 1, unit, 0)
        return 0

    lax.fori_loop(0, 4, stage, 0)

    is_cond = c == 0
    width = pos_ref.shape[1]
    patch = wpatch_ref[...].astype(f32)
    patch = jnp.where(is_cond, patch[:, 0:width], patch[:, width : 2 * width]).astype(bf16)
    t_now = time_ref[0]
    sigma_now = sigma_ref[t_now].astype(f32) / 1000.0
    sigma_next = sigma_ref[t_now + 1].astype(f32) / 1000.0

    def collect(t):
        j = lax.rem(x + 4 - STAGES[t], 4)
        for dz in range(4):
            for dl in range(2):
                if t + dz + dl == 0:
                    own_back.wait()
                else:
                    back_landed(t, STAGES[t], dz, dl).wait_recv()
        low = low_lanes(FIRST)
        for l in range(2):
            for pair in range(2):
                even = got[j * 2 + l, 2 * pair].astype(f32)
                odd = got[j * 2 + l, 2 * pair + 1].astype(f32)
                columns = pl.ds(l * 256 + pair * 128, 128)
                att[j, 0:FIRST, columns] = jnp.where(low, even, pltpu.roll(odd, HEAD, 1)).astype(bf16)
                rest = jnp.where(low, pltpu.roll(even, HEAD, 1), odd).astype(bf16)
                att[j, FIRST:ROWS, columns] = rest[2 * FIRST - ROWS : FIRST]

    def weights_there(t):
        i = (4 - STAGES[t]) % 4
        if i == 0:
            for copy in out_in:
                copy.wait()
        else:
            out_core(i, False, True).wait_recv()
        out_core(i, True, True).wait_recv()

    def partial(t):
        j = lax.rem(x + 4 - STAGES[t], 4)
        return jnp.dot(att[j], wo[j].reshape(4 * OUT_HALF, wo.shape[4]), preferred_element_type=f32)

    pass_out(2)
    for t in range(3):
        collect(t)
        weights_there(t)
    projected = partial(0) + partial(1) + partial(2)
    collect(3)
    weights_there(3)
    projected = projected + partial(3)
    mixed = hid_ref[0].astype(f32) + mod_ref[2] * projected
    final = (layer_norm(mixed) * (1.0 + mod_ref[4]) + mod_ref[3]).astype(bf16)
    velocity = lax.dot_general(
        wfinal_ref[...], final, (((1,), (1,)), ((), ())), preferred_element_type=f32
    )
    vel[0] = velocity
    exchange = remote(vel.at[0], vel.at[1], vsend.at[0], vrecv.at[0], other)
    exchange.start()

    for i in range(9):
        sends[i].wait_send()
    for d in (1, 2, 3):
        text_z(d).wait_send()
        out_x(d).wait_send()
        out_core(d, False).wait_send()
    for d in range(4):
        for e in (1, 2, 3):
            text_y(d, e).wait_send()
        for copy in out_z(d):
            copy.wait_send()
        out_core(d, True).wait_send()
    for t in range(4):
        for d in (1, 2, 3):
            copy_kv(t, d).wait_send()
            copy_q(t, d).wait_send()
        for d in range(4):
            for e in (1, 2, 3):
                copy_y(t, d, e).wait_send()
            for dl in range(2):
                if t + d + dl > 0:
                    back(t, STAGES[t], d, dl).wait_send()

    exchange.wait()
    others = vel[1]
    cond = jnp.where(is_cond, velocity, others)
    uncond = jnp.where(is_cond, others, velocity)
    guided = uncond + guidance * (cond - uncond)
    latent = lat_ref[...] + (sigma_next - sigma_now) * guided
    embedded = jnp.dot(latent.T.astype(bf16), patch, preferred_element_type=f32)
    next_ref[...] = (embedded + pos_ref[...].astype(f32)).astype(bf16)
    channels = guided_ref.shape[0]
    guided_ref[...] = jnp.where(is_cond, guided[0:channels], guided[channels:])
    latent_ref[...] = jnp.where(is_cond, latent[0:channels], latent[channels:])


def body(
    hidden, text_states, modulation, w_qkv, w_text, w_out, qk_gain, w_final, w_patch,
    position, latent, text_len, timestep, sigma_table,
):
    width = hidden.shape[2]
    channels = latent.shape[1] // 2
    vmem = pl.BlockSpec(memory_space=pltpu.VMEM)
    hbm = pl.BlockSpec(memory_space=pl.ANY)
    smem = pl.BlockSpec(memory_space=pltpu.SMEM)
    dma = pltpu.SemaphoreType.DMA
    guided, next_latent, next_hidden = pl.pallas_call(
        kernel,
        out_shape=[
            jax.ShapeDtypeStruct((channels, ROWS), f32),
            jax.ShapeDtypeStruct((channels, ROWS), f32),
            jax.ShapeDtypeStruct(position.shape, bf16),
        ],
        in_specs=[vmem, vmem, vmem, hbm, hbm, hbm, vmem, vmem, vmem, vmem, vmem, smem, smem, smem],
        out_specs=[vmem, vmem, vmem],
        scratch_shapes=[
            pltpu.VMEM((8, ROWS, width), bf16),
            pltpu.VMEM((3, width, 256), bf16),
            pltpu.VMEM((2, width, 256), bf16),
            pltpu.VMEM((TXT_PAD, width), bf16),
            pltpu.VMEM((4, 4, PAIR, 128), bf16),
            pltpu.VMEM((4, 4, ROWS, 128), bf16),
            pltpu.VMEM((4, TXT_PAD, 128), bf16),
            pltpu.VMEM((4, KEYS, 128), bf16),
            pltpu.VMEM((4, KEYS, 128), bf16),
            pltpu.VMEM((4, 4, ROWS, 128), bf16),
            pltpu.VMEM((4, QUERIES, 128), bf16),
            pltpu.VMEM((TXT_KEYS, 128), bf16),
            pltpu.VMEM((TXT_KEYS, 128), bf16),
            pltpu.VMEM((4, QUERIES, 1), f32),
            pltpu.VMEM((4, QUERIES, 128), f32),
            pltpu.VMEM((4, 8, FIRST, 128), bf16),
            pltpu.VMEM((8, 4, FIRST, 128), bf16),
            pltpu.VMEM((4, ROWS, 4 * OUT_HALF), bf16),
            pltpu.VMEM((4, 2, 2, OUT_HALF, width), bf16),
            pltpu.VMEM((2, 2 * channels, ROWS), f32),
            dma((7,)), dma((10,)),
            dma((9,)), dma((9,)),
            dma((4, 3)), dma((4, 3)),
            dma((4, 3)), dma((4, 3)),
            dma((4, 4, 3)), dma((4, 4, 3)),
            dma((3,)), dma((3,)),
            dma((4, 3)), dma((4, 3)),
            dma((3,)), dma((3,)),
            dma((4,)), dma((4,)), dma((4,)), dma((4,)),
            dma((4,)), dma((4,)), dma((4,)), dma((4,)),
            dma((4, 4, 2)), dma((4, 4, 2)),
            dma((1,)), dma((1,)),
        ],
        compiler_params=pltpu.CompilerParams(
            collective_id=0, has_side_effects=True, vmem_limit_bytes=60 << 20
        ),
        name="sublayer",
    )(
        hidden, text_states, jnp.swapaxes(modulation, 0, 1), w_qkv, w_text, w_out, qk_gain,
        w_final.T, w_patch, position, latent.T, text_len, timestep, sigma_table,
    )
    return guided.T, next_latent.T, next_hidden


def solution(mesh):
    in_specs = (
        P("cfg", ("blk", "uly"), None),
        P("cfg", "blk", None),
        P("cfg", None, None),
        P(None, None, "uly"),
        P(None, None, "uly"),
        P("uly", None),
        P(),
        P(),
        P(),
        P(("blk", "uly"), "cfg"),
        P(("blk", "uly"), None),
        P("cfg"),
        P(),
        P(),
    )
    out_specs = (P(("blk", "uly"), "cfg"), P(("blk", "uly"), "cfg"), P(("blk", "uly"), "cfg"))
    return jax.shard_map(body, mesh=mesh, in_specs=in_specs, out_specs=out_specs, check_vma=False)
```

time: 561 us -> 124 us (0.22)
  waiting for transfers between devices: 313 us -> 0 us
  Pallas kernels: 0 us -> 117 us
  matrix products: 112 us -> 0 us
  local copies, waits for them, and re-layouts: 79.3 us -> 4.27 us
  other arithmetic: 25.1 us -> 0 us
  between operations: 16.6 us -> 1.94 us
  starting transfers between devices: 12.4 us -> 0 us
    all_gather x5 -> x0, waiting for transfers between devices: 304 us -> none  [the longest x1 88.4 us: body(): value_rows = lax.all_gather(projected[2], 'blk', axis=0, tiled=True)]
    pallas_call x0 -> x1, Pallas kernels: none -> 117 us  [body(): pl.pallas_call(kernel, out_shape=[jax.ShapeDtypeStruct((channels, ROWS),...]
    dot_general x42 -> x0, matrix products: 112 us -> none  [the longest x16 68.9 us: fold_block(): jnp.einsum('hqk,khd->hqd', block_weights.astype(jnp.bfloat16), value_bloc...]
    while x48 -> x0, local copies, waits for them, and re-layouts: 42.6 us -> none
    dynamic_slice x49 -> x0, local copies, waits for them, and re-layouts: 25 us -> none  [the longest x48 24.4 us: body(): lax.scan(scan_step, (highest, totals, summed), (key_blocks, value_blocks))]
    reduce_sum x21 -> x0, other arithmetic: 21.4 us -> none  [the longest x16 17.3 us: fold_block(): new_total = run_total * shrink + jnp.sum(block_weights, axis=-1)]
    all_to_all x1 -> x0, starting transfers between devices: 11.2 us -> none  [body(): lax.all_to_all(attended, 'uly', split_axis=0, concat_axis=1, tiled=True)]
    all_to_all x1 -> x0, waiting for transfers between devices: 8.53 us -> none  [body(): lax.all_to_all(attended, 'uly', split_axis=0, concat_axis=1, tiled=True)]
  transfers between devices with their start and end apart: 7 -> 0, of which waited for: 6 -> 0; matrix products, arithmetic and copies ran while one was open for 29% -> 0% of each run, Pallas kernels for 0% -> 0%
where the time goes in v3:
time: 124 us; the launch traced here: 123 us
  Pallas kernels  117 us (94%)
  local copies, waits for them, and re-layouts  4.27 us (3%)
  between operations  1.94 us (2%)
    pallas_call x1, Pallas kernels, body(): pl.pallas_call(kernel, out_shape=[jax.ShapeDtypeStruct((channels, ROWS),...  117 us
    unnamed x3, local copies, waits for them, and re-layouts  4.27 us

profile of v3, /device:TPU:3, one launch (start us, length us, event | category | flops | bytes accessed | tf_op | source)
XLA Modules:
  0.0 123.4 jit_solution(7655022454674741771)
XLA Ops:
  1.9 117.2 %sublayer.1 = (f32[32,80]{1,0:T(8,128)}, f32[32,80]{1,0:T(8,128)}, bf16[80,1216]{1,0:T(8,128)(2,1)}) custom-call(bf16[1,80,2432]{2,1,0:T(8,128)(2,1)} %hid_ref.1, bf16[1,21,2432]{2,1,0:T(8,128)(2,1)} %txt_ref.1, f32[5,1,2432]{2,1,0:T(1,128)} %bitcast.6, bf16[3,2432,256]{2,1,0:T(8,128)(2,1)} %wqkv_ref.1, bf16[2,2432,256]{2,1,0:T(8,128)(2,1)} %wtext_ref.1, ...), custom_call_target="tpu_custom_call" | custom-call | tf_op jit(solution)/shard_map/sublayer/pallas_call | solution.py:557
  119.1 1.3 %copy.22 = f32[80,32]{0,1:T(8,128)} copy(f32[80,32]{0,1:T(8,128)} %bitcast.9) | data formatting | bytes 20480
  120.5 1.3 %copy.23 = f32[80,32]{0,1:T(8,128)} copy(f32[80,32]{0,1:T(8,128)} %bitcast.8) | data formatting | bytes 20480
  121.8 1.6 %copy.24 = bf16[80,1216]{1,0:T(8,128)(2,1)} copy(bf16[80,1216]{1,0:T(8,128)(2,1)} %get-tuple-element.14) | data formatting | bytes 389120

commit v4 on v3

--- a/solution.py
+++ b/solution.py
@@ -22,7 +22,7 @@
 QUERIES = 4 * PAIR
 FIRST = 48
 OUT_HALF = 128
-STAGES = (0, 3, 1, 2)
+STAGES = (((0, 0), (0, 1)), ((3, 0), (1, 0)), ((3, 1), (1, 1)), ((2, 0), (2, 1)))
 
 
 def layer_norm(values):
@@ -263,15 +263,22 @@
         out_core(i, True).start()
 
 
-    def back(t, dx, dz, dl):
-        src = ob.at[t, lax.rem(zh + dz, 4) * 2 + lax.rem(zl + dl, 2)]
-        return remote(src, got.at[u, zh], osend.at[t, dz, dl], orecv.at[t, dz, dl], at(dz=dz, dx=dx, dl=dl))
-
-    def back_landed(t, dx, dz, dl):
-        slot = got.at[lax.rem(x + 4 - dx, 4) * 2 + lax.rem(zl + dl, 2), lax.rem(zh + 4 - dz, 4)]
-        return remote(slot, slot, osend.at[t, dz, dl], orecv.at[t, dz, dl], at(dz=dz, dx=dx, dl=dl))
-
-    own_back = pltpu.make_async_copy(ob.at[0, zh * 2 + zl], got.at[u, zh], lsem.at[9])
+    def back(t, k, dz):
+        dx, dl = STAGES[t][k]
+        src = ob.at[t, lax.rem(zh + dz, 4) * 2 + k]
+        return remote(src, got.at[u, zh], osend.at[t, k, dz], orecv.at[t, k, dz], at(dz=dz, dx=dx, dl=dl))
+
+    def sender(t, k):
+        dx, dl = STAGES[t][k]
+        return lax.rem(x + 4 - dx, 4), lax.rem(zl + dl, 2)
+
+    def back_landed(t, k, dz):
+        dx, dl = STAGES[t][k]
+        j, l = sender(t, k)
+        slot = got.at[j * 2 + l, lax.rem(zh + 4 - dz, 4)]
+        return remote(slot, slot, osend.at[t, k, dz], orecv.at[t, k, dz], at(dz=dz, dx=dx, dl=dl))
+
+    own_back = pltpu.make_async_copy(ob.at[0, zh * 2], got.at[u, zh], lsem.at[9])
 
     for copy in text_in:
         copy.wait()
@@ -289,8 +296,9 @@
         copy.wait()
 
     def project(t):
-        p = lax.rem(x + STAGES[t], 4)
-        pair = mods[pl.ds(p * 2, 2)].reshape(PAIR, mods.shape[2])
+        pair = jnp.concatenate(
+            [mods[lax.rem(x + dx, 4) * 2 + lax.rem(zl + dl, 2)] for dx, dl in STAGES[t]], axis=0
+        )
         ks = head_norm(jnp.dot(pair, wq[1], preferred_element_type=f32), gain_k)
         vs = jnp.dot(pair, wq[2], preferred_element_type=f32)
         for h, value in enumerate(pack_heads(ks, [vs[:, 0:128], vs[:, 128:256]])):
@@ -321,28 +329,23 @@
     arrive[2].wait_recv()
     sends[6].start()
     project(0)
+    project(1)
     for d in (1, 2, 3):
         text_z_landed(d).wait_recv()
         for e in (1, 2, 3):
             text_y(d, e).start()
+    pass_on(0)
     arrive[3].wait_recv()
     sends[7].start()
     arrive[4].wait_recv()
     sends[8].start()
-    project(1)
-    pass_on(0)
     project(2)
+    pass_on(1)
     own_text.wait()
     for d in range(4):
         for e in (1, 2, 3):
             text_y_landed(d, e).wait_recv()
     tv1[...] = values_and_ones(tkv[...])
-    for i in (5, 6, 7, 8):
-        arrive[i].wait_recv()
-    out_x(1).start()
-    out_x(3).start()
-    project(3)
-    pass_on(1)
 
     def fold(carry, q, keys, values, usable):
         high, total = carry
@@ -350,7 +353,8 @@
         if usable is not None:
             scores = jnp.where(usable, scores, -1e30)
         new_high = jnp.maximum(high, jnp.max(scores, axis=1, keepdims=True))
-        weights = jnp.exp2(scores - new_high).astype(bf16)
+        wide = jnp.concatenate([new_high] * (keys.shape[0] // 128), axis=1)
+        weights = jnp.exp2(scores - wide).astype(bf16)
         shrink = jnp.exp2(high - new_high)
         return new_high, total * shrink + jnp.dot(weights, values, preferred_element_type=f32)
 
@@ -362,23 +366,12 @@
     def stage(s, _):
         @pl.when(s == 1)
         def _():
+            for i in (5, 6, 7, 8):
+                arrive[i].wait_recv()
+            out_x(1).start()
+            out_x(3).start()
+            project(3)
             pass_on(2)
-            start_out_z(0)
-            out_x(2).start()
-
-        @pl.when(s == 2)
-        def _():
-            for i in (1, 3):
-                out_x_landed(i).wait_recv()
-            for i in (1, 3):
-                start_out_z(i)
-                out_core(i, False).start()
-
-        @pl.when(s == 3)
-        def _():
-            out_x_landed(2).wait_recv()
-            start_out_z(2)
-            out_core(2, False).start()
 
         own_q(s).wait()
         for d in (1, 2, 3):
@@ -390,7 +383,7 @@
             q2[s, PAIR * p + ROWS : PAIR * p + PAIR, :] = jnp.where(
                 low, pltpu.roll(packed, HEAD, 1), 0.0
             ).astype(bf16)
-        first = (jnp.full((QUERIES, 1), -1e30, f32), jnp.zeros((QUERIES, 128), f32))
+        first = (jnp.full((QUERIES, 128), -1e30, f32), jnp.zeros((QUERIES, 128), f32))
         top[s], acc[s] = fold(first, q2[s], tkv[...], tv1[...], usable)
         own_kv(s).wait()
         for d in range(4):
@@ -409,15 +402,31 @@
             top[i] = high
             acc[i] = total
 
-            @pl.when(jnp.logical_and(s == 1, j == 0))
+            @pl.when(jnp.logical_and(s == 1, j == 1))
             def _():
                 pass_on(3)
+                start_out_z(0)
+                out_x(2).start()
+
+            @pl.when(jnp.logical_and(s == 2, j == 1))
+            def _():
+                for i in (1, 3):
+                    out_x_landed(i).wait_recv()
+                for i in (1, 3):
+                    start_out_z(i)
+                    out_core(i, False).start()
 
             @pl.when(jnp.logical_and(s == 2, j == 3))
             def _():
                 pass_out(0)
 
-            @pl.when(jnp.logical_and(s == 3, j == 3))
+            @pl.when(jnp.logical_and(s == 3, j == 1))
+            def _():
+                out_x_landed(2).wait_recv()
+                start_out_z(2)
+                out_core(2, False).start()
+
+            @pl.when(jnp.logical_and(s == 3, j == 4))
             def _():
                 pass_out(1)
                 pass_out(3)
@@ -439,11 +448,11 @@
                     @pl.when(i == t)
                     def _():
                         for dz in (2, 1, 3, 0):
-                            for dl in range(2):
-                                if t + dz + dl == 0:
+                            for k in range(2):
+                                if t + k + dz == 0:
                                     own_back.start()
                                 else:
-                                    back(t, STAGES[t], dz, dl).start()
+                                    back(t, k, dz).start()
 
             return 0
 
@@ -461,35 +470,41 @@
     sigma_next = sigma_ref[t_now + 1].astype(f32) / 1000.0
 
     def collect(t):
-        j = lax.rem(x + 4 - STAGES[t], 4)
-        for dz in range(4):
-            for dl in range(2):
-                if t + dz + dl == 0:
+        low = low_lanes(FIRST)
+        for k in range(2):
+            for dz in range(4):
+                if t + k + dz == 0:
                     own_back.wait()
                 else:
-                    back_landed(t, STAGES[t], dz, dl).wait_recv()
-        low = low_lanes(FIRST)
-        for l in range(2):
+                    back_landed(t, k, dz).wait_recv()
+            j, l = sender(t, k)
+            n = j * 2 + l
             for pair in range(2):
-                even = got[j * 2 + l, 2 * pair].astype(f32)
-                odd = got[j * 2 + l, 2 * pair + 1].astype(f32)
-                columns = pl.ds(l * 256 + pair * 128, 128)
-                att[j, 0:FIRST, columns] = jnp.where(low, even, pltpu.roll(odd, HEAD, 1)).astype(bf16)
+                even = got[n, 2 * pair].astype(f32)
+                odd = got[n, 2 * pair + 1].astype(f32)
+                columns = pl.ds(pair * 128, 128)
+                att[n, 0:FIRST, columns] = jnp.where(low, even, pltpu.roll(odd, HEAD, 1)).astype(bf16)
                 rest = jnp.where(low, pltpu.roll(even, HEAD, 1), odd).astype(bf16)
-                att[j, FIRST:ROWS, columns] = rest[2 * FIRST - ROWS : FIRST]
+                att[n, FIRST:ROWS, columns] = rest[2 * FIRST - ROWS : FIRST]
 
     def weights_there(t):
-        i = (4 - STAGES[t]) % 4
-        if i == 0:
-            for copy in out_in:
-                copy.wait()
-        else:
-            out_core(i, False, True).wait_recv()
-        out_core(i, True, True).wait_recv()
+        for dx, dl in STAGES[t]:
+            i = (4 - dx) % 4
+            if dl == 1:
+                out_core(i, True, True).wait_recv()
+            elif i > 0:
+                out_core(i, False, True).wait_recv()
+            else:
+                for copy in out_in:
+                    copy.wait()
 
     def partial(t):
-        j = lax.rem(x + 4 - STAGES[t], 4)
-        return jnp.dot(att[j], wo[j].reshape(4 * OUT_HALF, wo.shape[4]), preferred_element_type=f32)
+        total = 0.0
+        for k in range(2):
+            j, l = sender(t, k)
+            weights = wo[j, l].reshape(2 * OUT_HALF, wo.shape[4])
+            total += jnp.dot(att[j * 2 + l], weights, preferred_element_type=f32)
+        return total
 
     pass_out(2)
     for t in range(3):
@@ -527,9 +542,9 @@
         for d in range(4):
             for e in (1, 2, 3):
                 copy_y(t, d, e).wait_send()
-            for dl in range(2):
-                if t + d + dl > 0:
-                    back(t, STAGES[t], d, dl).wait_send()
+            for k in range(2):
+                if t + k + d > 0:
+                    back(t, k, d).wait_send()
 
     exchange.wait()
     others = vel[1]
@@ -577,11 +592,11 @@
             pltpu.VMEM((4, QUERIES, 128), bf16),
             pltpu.VMEM((TXT_KEYS, 128), bf16),
             pltpu.VMEM((TXT_KEYS, 128), bf16),
-            pltpu.VMEM((4, QUERIES, 1), f32),
+            pltpu.VMEM((4, QUERIES, 128), f32),
             pltpu.VMEM((4, QUERIES, 128), f32),
             pltpu.VMEM((4, 8, FIRST, 128), bf16),
             pltpu.VMEM((8, 4, FIRST, 128), bf16),
-            pltpu.VMEM((4, ROWS, 4 * OUT_HALF), bf16),
+            pltpu.VMEM((8, ROWS, 2 * OUT_HALF), bf16),
             pltpu.VMEM((4, 2, 2, OUT_HALF, width), bf16),
             pltpu.VMEM((2, 2 * channels, ROWS), f32),
             dma((7,)), dma((10,)),
@@ -594,7 +609,7 @@
             dma((3,)), dma((3,)),
             dma((4,)), dma((4,)), dma((4,)), dma((4,)),
             dma((4,)), dma((4,)), dma((4,)), dma((4,)),
-            dma((4, 4, 2)), dma((4, 4, 2)),
+            dma((4, 2, 4)), dma((4, 2, 4)),
             dma((1,)), dma((1,)),
         ],
         compiler_params=pltpu.CompilerParams(

time: 124 us -> 110 us (0.89)
  Pallas kernels: 117 us -> 104 us
    pallas_call x1, Pallas kernels: 117 us -> 104 us  [body(): pl.pallas_call(kernel, out_shape=[jax.ShapeDtypeStruct((channels, ROWS),...]
where the time goes in v4:
time: 110 us
  Pallas kernels  104 us (95%)
  local copies, waits for them, and re-layouts  4.27 us (4%)
  between operations  1.94 us (2%)
    pallas_call x1, Pallas kernels, body(): pl.pallas_call(kernel, out_shape=[jax.ShapeDtypeStruct((channels, ROWS),...  104 us
    unnamed x3, local copies, waits for them, and re-layouts  4.27 us

profile of v4, /device:TPU:3, one launch (start us, length us, event | category | flops | bytes accessed | tf_op | source)
XLA Modules:
  0.0 110.1 jit_solution(15477368347537825534)
XLA Ops:
  1.9 103.9 %sublayer.1 = (f32[32,80]{1,0:T(8,128)}, f32[32,80]{1,0:T(8,128)}, bf16[80,1216]{1,0:T(8,128)(2,1)}) custom-call(bf16[1,80,2432]{2,1,0:T(8,128)(2,1)} %hid_ref.1, bf16[1,21,2432]{2,1,0:T(8,128)(2,1)} %txt_ref.1, f32[5,1,2432]{2,1,0:T(1,128)} %bitcast.6, bf16[3,2432,256]{2,1,0:T(8,128)(2,1)} %wqkv_ref.1, bf16[2,2432,256]{2,1,0:T(8,128)(2,1)} %wtext_ref.1, ...), custom_call_target="tpu_custom_call" | custom-call | tf_op jit(solution)/shard_map/sublayer/pallas_call | solution.py:572
  105.8 1.3 %copy.22 = f32[80,32]{0,1:T(8,128)} copy(f32[80,32]{0,1:T(8,128)} %bitcast.9) | data formatting | bytes 20480
  107.2 1.3 %copy.23 = f32[80,32]{0,1:T(8,128)} copy(f32[80,32]{0,1:T(8,128)} %bitcast.8) | data formatting | bytes 20480
  108.5 1.6 %copy.24 = bf16[80,1216]{1,0:T(8,128)(2,1)} copy(bf16[80,1216]{1,0:T(8,128)(2,1)} %get-tuple-element.14) | data formatting | bytes 389120

commit v5 on v4

--- a/solution.py
+++ b/solution.py
@@ -88,6 +88,7 @@
     partner, up, down = at(dl=1), at(dx=1), at(dx=3)
     above = (c, lax.rem(zh + zl, 4) * 4 + y, x * 2 + 1 - zl)
     below = (c, lax.rem(zh + 3 + zl, 4) * 4 + y, x * 2 + 1 - zl)
+    far = (c, lax.rem(zh + 3 + 2 * zl, 4) * 4 + y, x * 2 + 1 - zl)
 
     qkv_in = [pltpu.make_async_copy(wqkv_ref.at[i], wq.at[i], wsem.at[i]) for i in range(3)]
     text_in = [pltpu.make_async_copy(wtext_ref.at[i], wt.at[i], wsem.at[3 + i]) for i in range(2)]
@@ -228,19 +229,34 @@
 
     half = OUT_HALF // 2
 
+    def out_x_on(k):
+        dx, to = ((3, up), (1, down))[k]
+        ref = wo.at[lax.rem(x + dx, 4), zl, c, pl.ds(half * k, half)]
+        return remote(ref, ref, xsend.at[1 + 2 * k], xrecv.at[1 + 2 * k], to)
+
+    def out_x_on_landed(k):
+        ref = wo.at[lax.rem(x + 2, 4), zl, c, pl.ds(half * k, half)]
+        return remote(ref, ref, xsend.at[1 + 2 * k], xrecv.at[1 + 2 * k], (up, down)[k])
+
+    def out_far():
+        src = wout_ref.at[pl.ds(pl.multiple_of(c * OUT_HALF, OUT_HALF), OUT_HALF)]
+        return remote(src, wo.at[x, zl, c], usend.at[0], urecv.at[0], far)
+
     def out_z(i):
+        if i == 0:
+            return [out_far()]
         j = lax.rem(x + i, 4)
         copies = []
         for k, to, send, recv in ((0, above, usend, urecv), (1, below, dsend, drecv)):
             ref = wo.at[j, zl, c, pl.ds(half * k, half)]
-            src = ref
-            if i == 0:
-                src = wout_ref.at[pl.ds(pl.multiple_of(c * OUT_HALF + half * k, half), half)]
-            copies.append(remote(src, ref, send.at[i], recv.at[i], to))
+            copies.append(remote(ref, ref, send.at[i], recv.at[i], to))
         return copies
 
     def out_z_landed(i):
         j = lax.rem(x + i, 4)
+        if i == 0:
+            ref = wo.at[x, 1 - zl, c]
+            return [remote(ref, ref, usend.at[0], urecv.at[0], far)]
         copies = []
         for k, to, send, recv in ((0, above, usend, urecv), (1, below, dsend, drecv)):
             ref = wo.at[j, 1 - zl, c, pl.ds(half * k, half)]
@@ -405,24 +421,23 @@
             @pl.when(jnp.logical_and(s == 1, j == 1))
             def _():
                 pass_on(3)
-                start_out_z(0)
-                out_x(2).start()
-
-            @pl.when(jnp.logical_and(s == 2, j == 1))
+                out_far().start()
+
+            @pl.when(jnp.logical_and(s == 2, j == 2))
             def _():
                 for i in (1, 3):
                     out_x_landed(i).wait_recv()
+                for k in (0, 1):
+                    out_x_on(k).start()
                 for i in (1, 3):
                     start_out_z(i)
                     out_core(i, False).start()
 
-            @pl.when(jnp.logical_and(s == 2, j == 3))
+            @pl.when(jnp.logical_and(s == 3, j == 0))
             def _():
                 pass_out(0)
-
-            @pl.when(jnp.logical_and(s == 3, j == 1))
-            def _():
-                out_x_landed(2).wait_recv()
+                for k in (0, 1):
+                    out_x_on_landed(k).wait_recv()
                 start_out_z(2)
                 out_core(2, False).start()
 
@@ -527,8 +542,11 @@
         sends[i].wait_send()
     for d in (1, 2, 3):
         text_z(d).wait_send()
-        out_x(d).wait_send()
+        if d != 2:
+            out_x(d).wait_send()
         out_core(d, False).wait_send()
+    for k in (0, 1):
+        out_x_on(k).wait_send()
     for d in range(4):
         for e in (1, 2, 3):
             text_y(d, e).wait_send()
@@ -606,7 +624,7 @@
             dma((4, 4, 3)), dma((4, 4, 3)),
             dma((3,)), dma((3,)),
             dma((4, 3)), dma((4, 3)),
-            dma((3,)), dma((3,)),
+            dma((4,)), dma((4,)),
             dma((4,)), dma((4,)), dma((4,)), dma((4,)),
             dma((4,)), dma((4,)), dma((4,)), dma((4,)),
             dma((4, 2, 4)), dma((4, 2, 4)),

time: 110 us -> 106 us (0.964); the launches traced: 110 us -> 105 us
  Pallas kernels: 104 us -> 98.5 us
    pallas_call x1, Pallas kernels: 104 us -> 98.5 us  [body(): pl.pallas_call(kernel, out_shape=[jax.ShapeDtypeStruct((channels, ROWS),...]
where the time goes in v5:
time: 106 us; the launch traced here: 105 us
  Pallas kernels  98.5 us (93%)
  local copies, waits for them, and re-layouts  4.27 us (4%)
  between operations  1.94 us (2%)
    pallas_call x1, Pallas kernels, body(): pl.pallas_call(kernel, out_shape=[jax.ShapeDtypeStruct((channels, ROWS),...  98.5 us
    unnamed x3, local copies, waits for them, and re-layouts  4.27 us

profile of v5, /device:TPU:3, one launch (start us, length us, event | category | flops | bytes accessed | tf_op | source)
XLA Modules:
  0.0 104.7 jit_solution(394834861042361206)
XLA Ops:
  1.9 98.5 %sublayer.1 = (f32[32,80]{1,0:T(8,128)}, f32[32,80]{1,0:T(8,128)}, bf16[80,1216]{1,0:T(8,128)(2,1)}) custom-call(bf16[1,80,2432]{2,1,0:T(8,128)(2,1)} %hid_ref.1, bf16[1,21,2432]{2,1,0:T(8,128)(2,1)} %txt_ref.1, f32[5,1,2432]{2,1,0:T(1,128)} %bitcast.6, bf16[3,2432,256]{2,1,0:T(8,128)(2,1)} %wqkv_ref.1, bf16[2,2432,256]{2,1,0:T(8,128)(2,1)} %wtext_ref.1, ...), custom_call_target="tpu_custom_call" | custom-call | tf_op jit(solution)/shard_map/sublayer/pallas_call | solution.py:590
  100.4 1.3 %copy.22 = f32[80,32]{0,1:T(8,128)} copy(f32[80,32]{0,1:T(8,128)} %bitcast.9) | data formatting | bytes 20480
  101.7 1.3 %copy.23 = f32[80,32]{0,1:T(8,128)} copy(f32[80,32]{0,1:T(8,128)} %bitcast.8) | data formatting | bytes 20480
  103.1 1.6 %copy.24 = bf16[80,1216]{1,0:T(8,128)(2,1)} copy(bf16[80,1216]{1,0:T(8,128)(2,1)} %get-tuple-element.14) | data formatting | bytes 389120

commit v6 on v5

--- a/solution.py
+++ b/solution.py
@@ -66,7 +66,7 @@
 def kernel(
     hid_ref, txt_ref, mod_ref, wqkv_ref, wtext_ref, wout_ref, gain_ref, wfinal_ref, wpatch_ref,
     pos_ref, lat_ref, len_ref, time_ref, sigma_ref,
-    guided_ref, latent_ref, next_ref,
+    both_ref, next_ref,
     mods, wq, wt, txt, kvst, qst, tst, kvb, v1, qb, q2, tkv, tv1, top, acc, ob, got, att, wo, vel,
     wsem, lsem, bsend, brecv, zsend, zrecv, qsend, qrecv, ysend, yrecv,
     tzsend, tzrecv, tysend, tyrecv, xsend, xrecv, usend, urecv, dsend, drecv,
@@ -438,12 +438,15 @@
                 pass_out(0)
                 for k in (0, 1):
                     out_x_on_landed(k).wait_recv()
-                start_out_z(2)
+                    out_z(2)[k].start()
                 out_core(2, False).start()
+
+            @pl.when(jnp.logical_and(s == 3, j == 3))
+            def _():
+                pass_out(1)
 
             @pl.when(jnp.logical_and(s == 3, j == 4))
             def _():
-                pass_out(1)
                 pass_out(3)
 
             @pl.when(jnp.logical_and(s == 3, jnp.logical_or(j < 3, j == 6)))
@@ -521,11 +524,14 @@
             total += jnp.dot(att[j * 2 + l], weights, preferred_element_type=f32)
         return total
 
+    collect(0)
+    weights_there(0)
+    projected = partial(0)
     pass_out(2)
-    for t in range(3):
+    for t in (1, 2):
         collect(t)
         weights_there(t)
-    projected = partial(0) + partial(1) + partial(2)
+    projected = projected + partial(1) + partial(2)
     collect(3)
     weights_there(3)
     projected = projected + partial(3)
@@ -572,9 +578,9 @@
     latent = lat_ref[...] + (sigma_next - sigma_now) * guided
     embedded = jnp.dot(latent.T.astype(bf16), patch, preferred_element_type=f32)
     next_ref[...] = (embedded + pos_ref[...].astype(f32)).astype(bf16)
-    channels = guided_ref.shape[0]
-    guided_ref[...] = jnp.where(is_cond, guided[0:channels], guided[channels:])
-    latent_ref[...] = jnp.where(is_cond, latent[0:channels], latent[channels:])
+    channels = both_ref.shape[1]
+    both_ref[0] = jnp.where(is_cond, guided[0:channels], guided[channels:])
+    both_ref[1] = jnp.where(is_cond, latent[0:channels], latent[channels:])
 
 
 def body(
@@ -587,15 +593,14 @@
     hbm = pl.BlockSpec(memory_space=pl.ANY)
     smem = pl.BlockSpec(memory_space=pltpu.SMEM)
     dma = pltpu.SemaphoreType.DMA
-    guided, next_latent, next_hidden = pl.pallas_call(
+    both, next_hidden = pl.pallas_call(
         kernel,
         out_shape=[
-            jax.ShapeDtypeStruct((channels, ROWS), f32),
-            jax.ShapeDtypeStruct((channels, ROWS), f32),
+            jax.ShapeDtypeStruct((2, channels, ROWS), f32),
             jax.ShapeDtypeStruct(position.shape, bf16),
         ],
         in_specs=[vmem, vmem, vmem, hbm, hbm, hbm, vmem, vmem, vmem, vmem, vmem, smem, smem, smem],
-        out_specs=[vmem, vmem, vmem],
+        out_specs=[vmem, vmem],
         scratch_shapes=[
             pltpu.VMEM((8, ROWS, width), bf16),
             pltpu.VMEM((3, width, 256), bf16),
@@ -638,7 +643,7 @@
         hidden, text_states, jnp.swapaxes(modulation, 0, 1), w_qkv, w_text, w_out, qk_gain,
         w_final.T, w_patch, position, latent.T, text_len, timestep, sigma_table,
     )
-    return guided.T, next_latent.T, next_hidden
+    return both[0].T, both[1].T, next_hidden
 
 
 def solution(mesh):

time: 106 us -> 104 us (0.981)
  local copies, waits for them, and re-layouts: 4.27 us -> 2.97 us
    unnamed x3 -> x1, local copies, waits for them, and re-layouts: 4.27 us -> 1.62 us
    transpose x0 -> x1, local copies, waits for them, and re-layouts: none -> 1.35 us  [body(): return (both[0].T, both[1].T, next_hidden)]
where the time goes in v6:
time: 104 us; the launch traced here: 103 us
  Pallas kernels  98.2 us (94%)
  local copies, waits for them, and re-layouts  2.97 us (3%)
  between operations  1.94 us (2%)
    pallas_call x1, Pallas kernels, body(): pl.pallas_call(kernel, out_shape=[jax.ShapeDtypeStruct((2, channels, ROWS...  98.2 us

profile of v6, /device:TPU:3, one launch (start us, length us, event | category | flops | bytes accessed | tf_op | source)
XLA Modules:
  0.0 103.1 jit_solution(14347999518209464634)
XLA Ops:
  1.9 98.2 %sublayer.1 = (f32[2,32,80]{2,1,0:T(8,128)}, bf16[80,1216]{1,0:T(8,128)(2,1)}) custom-call(bf16[1,80,2432]{2,1,0:T(8,128)(2,1)} %hid_ref.1, bf16[1,21,2432]{2,1,0:T(8,128)(2,1)} %txt_ref.1, f32[5,1,2432]{2,1,0:T(1,128)} %bitcast.12, bf16[3,2432,256]{2,1,0:T(8,128)(2,1)} %wqkv_ref.1, bf16[2,2432,256]{2,1,0:T(8,128)(2,1)} %wtext_ref.1, ...), custom_call_target="tpu_custom_call" | custom-call | tf_op jit(solution)/shard_map/sublayer/pallas_call | solution.py:596
  100.1 1.3 %slice_bitcast_fusion = (f32[80,32]{0,1:T(8,128)}, f32[80,32]{0,1:T(8,128)}) fusion(f32[2,32,80]{2,1,0:T(8,128)} %get-tuple-element.5), kind=kLoop, calls=%fused_computation | loop fusion | bytes 40960 | tf_op jit(solution)/shard_map/transpose | solution.py:646
  101.5 1.6 %copy.20 = bf16[80,1216]{1,0:T(8,128)(2,1)} copy(bf16[80,1216]{1,0:T(8,128)(2,1)} %get-tuple-element.14) | data formatting | bytes 389120
